TPU v7x, 32 devices: a whole 2x2x4 slice. The times are simulated.
32 devices in a mesh: rep: 8 (over y, x, core), shard: 4 (over z).
Axes of the slice: x: 2, y: 2, z: 4, core: 2. Of those that a mesh axis runs over, the one named last changes fastest.
Arguments:
- tokens: bfloat16 [8192, 1024], P(('rep', 'shard')), may hold values from -6 to 6
- sequence_start: int32 [8192], P(('rep', 'shard')), may hold values from 0 to 255, as said below
- routes: int32 [8192, 8], P(('rep', 'shard')), may hold values from 0 to 15, all different within a row; in each aligned block of 256 rows (0 to 255, 256 to 511, ...) at most 160 rows name the same one
- route_weights: float32 [8192, 8], P(('rep', 'shard')), may hold values from 0.05 to 0.3
- cotangent: bfloat16 [8192, 1024], P(('rep', 'shard')), may hold values from -6 to 6
- query_proj: bfloat16 [1024, 1024], P('shard'), may hold values from -0.1875 to 0.1875
- key_proj: bfloat16 [1024, 512], P('shard'), may hold values from -0.1875 to 0.1875
- value_proj: bfloat16 [1024, 512], P('shard'), may hold values from -0.1875 to 0.1875
- out_proj: bfloat16 [1024, 1024], P('shard'), may hold values from -1.5 to 1.5
- prenorm: bfloat16 [1024], P('shard'), may hold values from 0.5 to 1.5
- midnorm: bfloat16 [1024], P('shard'), may hold values from 0.5 to 1.5
- gate_proj: bfloat16 [16, 1024, 512], P('shard'), may hold values from -0.1875 to 0.1875
- up_proj: bfloat16 [16, 1024, 512], P('shard'), may hold values from -0.1875 to 0.1875
- down_proj: bfloat16 [16, 512, 1024], P('shard'), may hold values from -0.25 to 0.25
- query_moment: float32 [1024, 1024], P('shard'), may hold values from -640 to 640
- key_moment: float32 [1024, 512], P('shard'), may hold values from -640 to 640
- value_moment: float32 [1024, 512], P('shard'), may hold values from -640 to 640
- out_moment: float32 [1024, 1024], P('shard'), may hold values from -640 to 640
- prenorm_moment: float32 [1024], P('shard'), may hold values from -1792 to 1792
- midnorm_moment: float32 [1024], P('shard'), may hold values from -320 to 320
- gate_moment: float32 [16, 1024, 512], P('shard'), may hold values from -128 to 128
- up_moment: float32 [16, 1024, 512], P('shard'), may hold values from -128 to 128
- down_moment: float32 [16, 512, 1024], P('shard'), may hold values from -128 to 128
Outputs:
- mixed: bfloat16 [8192, 1024], P(('rep', 'shard'))
- grad_tokens: float32 [8192, 1024], P(('rep', 'shard'))
- query_grad: float32 [1024, 1024], P('shard')
- query_next: float32 [1024, 1024], P('shard')
- query_update: float32 [1024, 1024], P('shard')
- key_grad: float32 [1024, 512], P('shard')
- key_next: float32 [1024, 512], P('shard')
- key_update: float32 [1024, 512], P('shard')
- value_grad: float32 [1024, 512], P('shard')
- value_next: float32 [1024, 512], P('shard')
- value_update: float32 [1024, 512], P('shard')
- out_grad: float32 [1024, 1024], P('shard')
- out_next: float32 [1024, 1024], P('shard')
- out_update: float32 [1024, 1024], P('shard')
- prenorm_grad: float32 [1024], P('shard')
- prenorm_next: float32 [1024], P('shard')
- prenorm_update: float32 [1024], P('shard')
- midnorm_grad: float32 [1024], P('shard')
- midnorm_next: float32 [1024], P('shard')
- midnorm_update: float32 [1024], P('shard')
- gate_grad: float32 [16, 1024, 512], P('shard')
- gate_next: float32 [16, 1024, 512], P('shard')
- gate_update: float32 [16, 1024, 512], P('shard')
- up_grad: float32 [16, 1024, 512], P('shard')
- up_next: float32 [16, 1024, 512], P('shard')
- up_update: float32 [16, 1024, 512], P('shard')
- down_grad: float32 [16, 512, 1024], P('shard')
- down_next: float32 [16, 512, 1024], P('shard')
- down_update: float32 [16, 512, 1024], P('shard')
Inputs may be any that keep to these rules, and one draw needn't show every extreme that they name: `sequence_start`: within each device's block of 256 tokens, sequences are contiguous runs; every token holds the block-local index of its run's first token, which holds its own index. Some block is one sequence of all 256 tokens. `routes`: each token names 8 different experts. Among the rows of one device no expert is named by more than 160 rows, and in some device one expert is named by exactly 160.
All inputs are finite; a program needn't handle non-finite values.
Results may differ from a plain program's by a relative error of at most 0.011.
The roundings to bfloat16 on the way count: a program that leaves them out, or rounds other values in their place, can miss the bound.
Values may be sent and summed in bfloat16 or wider, within the bound.
A program may use at most 320 MiB of HBM per device.

v0:
```python
import math

import jax
import jax.numpy as jnp
from jax import lax
from jax.sharding import PartitionSpec as P

NHEADS = 16
KVHEADS = 8
HEAD = 64
TOPK = 8
EXPERTS = 16
NS_ITERS = 2
CAP = 160
BLOCK = 256


norm_epsilon = 1e-06
rotary_base = 10000.0
momentum_keep = 0.9
rate_matrix = 0.5
rate_gain = 0.0002
newton_first = 3.4445
newton_second = -4.775
newton_third = 2.0315
masked_score = -1e30
highest = lax.Precision.HIGHEST


def root_scale(values):
    inverse = lax.rsqrt(jnp.mean(values * values, axis=-1, keepdims=True) + norm_epsilon)
    return (values * inverse, inverse)


def root_back(grad_normed, scaling, scaled, inverse):
    grad_scaled = grad_normed * scaling
    inner_mean = jnp.mean(grad_scaled * scaled, axis=-1, keepdims=True)
    return (inverse * (grad_scaled - scaled * inner_mean), jnp.sum(grad_normed * scaled, axis=0))


def rotary_tables(positions):
    half_size = HEAD // 2
    frequency = rotary_base ** (-(jnp.arange(half_size, dtype=jnp.float32) * 2.0) / HEAD)
    angles = positions.astype(jnp.float32)[:, None] * frequency[None, :]
    angles = jnp.concatenate([angles, angles], axis=-1)
    return (jnp.cos(angles)[:, None, :], jnp.sin(angles)[:, None, :])


def rotate_half(values):
    half_size = values.shape[-1] // 2
    return jnp.concatenate([-values[..., half_size:], values[..., :half_size]], axis=-1)


def rotate_back(values):
    half_size = values.shape[-1] // 2
    return jnp.concatenate([values[..., half_size:], -values[..., :half_size]], axis=-1)


def block_scores(query_block, rotated_keys, start_block, sequence_start, offset):
    scores = jnp.einsum(
        "qkgd,tkd->kgqt", query_block, rotated_keys, preferred_element_type=jnp.float32
    ) * (1.0 / math.sqrt(HEAD))
    key_places = jnp.arange(rotated_keys.shape[0], dtype=jnp.int32)
    query_places = offset + jnp.arange(query_block.shape[0], dtype=jnp.int32)
    allowed = (start_block[:, None] == sequence_start[None, :]) & (
        key_places[None, :] <= query_places[:, None]
    )
    return jnp.where(allowed, scores, masked_score)


def attend_forward(queries, rotated_keys, values, sequence_start):
    block_count = queries.shape[0] // BLOCK

    def one_block(pieces):
        query_block, start_block, offset = pieces
        scores = block_scores(query_block, rotated_keys, start_block, sequence_start, offset)
        row_max = jnp.max(scores, axis=-1, keepdims=True)
        exponents = jnp.exp(scores - row_max)
        totals = jnp.sum(exponents, axis=-1, keepdims=True)
        softmax_low = (exponents / totals).astype(jnp.bfloat16)
        attended = jnp.einsum(
            "kgqt,tkd->qkgd", softmax_low, values, preferred_element_type=jnp.float32
        )
        return (attended, row_max + jnp.log(totals))

    shaped = queries.reshape((block_count, BLOCK) + queries.shape[1:])
    offsets = jnp.arange(block_count, dtype=jnp.int32) * BLOCK
    attended, log_total = lax.map(
        one_block, (shaped, sequence_start.reshape(block_count, BLOCK), offsets)
    )
    return (attended.reshape(queries.shape[0], -1), log_total)


def attend_backward(queries, rotated_keys, values, sequence_start, log_total, grad_heads):
    block_count = queries.shape[0] // BLOCK
    score_scale = 1.0 / math.sqrt(HEAD)

    def one_block(running, pieces):
        grad_keys, grad_values = running
        query_block, start_block, offset, log_block, grad_block = pieces
        scores = block_scores(query_block, rotated_keys, start_block, sequence_start, offset)
        softmax_full = jnp.exp(scores - log_block)
        grad_softmax = jnp.einsum(
            "qkgd,tkd->kgqt", grad_block, values, preferred_element_type=jnp.float32
        )
        inner_sum = jnp.sum(softmax_full * grad_softmax, axis=-1, keepdims=True)
        grad_scores = (softmax_full * (grad_softmax - inner_sum)).astype(jnp.bfloat16)
        grad_query = (
            jnp.einsum(
                "kgqt,tkd->qkgd", grad_scores, rotated_keys, preferred_element_type=jnp.float32
            )
            * score_scale
        )
        grad_keys = (
            grad_keys
            + jnp.einsum(
                "kgqt,qkgd->tkd", grad_scores, query_block, preferred_element_type=jnp.float32
            )
            * score_scale
        )
        grad_values = grad_values + jnp.einsum(
            "kgqt,qkgd->tkd",
            softmax_full.astype(jnp.bfloat16),
            grad_block,
            preferred_element_type=jnp.float32,
        )
        return ((grad_keys, grad_values), grad_query)

    shaped = queries.reshape((block_count, BLOCK) + queries.shape[1:])
    grad_shaped = grad_heads.reshape((block_count, BLOCK) + queries.shape[1:])
    offsets = jnp.arange(block_count, dtype=jnp.int32) * BLOCK
    key_zeros = jnp.zeros(rotated_keys.shape, jnp.float32)
    finals, grad_queries = lax.scan(
        one_block,
        (key_zeros, key_zeros),
        (shaped, sequence_start.reshape(block_count, BLOCK), offsets, log_total, grad_shaped),
    )
    return (grad_queries.reshape(queries.shape), finals[0], finals[1])


def expert_forward(routed, gate_weight, up_weight, down_weight):
    gate_linear = jnp.einsum(
        "gxcd,xdf->gxcf", routed, gate_weight, preferred_element_type=jnp.float32
    )
    up_linear = jnp.einsum("gxcd,xdf->gxcf", routed, up_weight, preferred_element_type=jnp.float32)
    hidden = (jax.nn.silu(gate_linear) * up_linear).astype(jnp.bfloat16)
    expert_out = jnp.einsum(
        "gxcf,xfd->gxcd", hidden, down_weight, preferred_element_type=jnp.float32
    ).astype(jnp.bfloat16)
    return (gate_linear, up_linear, hidden, expert_out)


def expert_backward(
    routed, gate_linear, up_linear, hidden, grad_out, gate_weight, up_weight, down_weight
):
    grad_hidden = jnp.einsum(
        "gxcd,xfd->gxcf", grad_out, down_weight, preferred_element_type=jnp.float32
    )
    down_sum = jnp.einsum("gxcf,gxcd->xfd", hidden, grad_out, preferred_element_type=jnp.float32)
    gate_sigmoid = jax.nn.sigmoid(gate_linear)
    gate_delta = (
        grad_hidden * up_linear * gate_sigmoid * (1.0 + gate_linear * (1.0 - gate_sigmoid))
    ).astype(jnp.bfloat16)
    up_delta = (grad_hidden * gate_linear * gate_sigmoid).astype(jnp.bfloat16)
    grad_routed = (
        jnp.einsum("gxcf,xdf->gxcd", gate_delta, gate_weight, preferred_element_type=jnp.float32)
        + jnp.einsum("gxcf,xdf->gxcd", up_delta, up_weight, preferred_element_type=jnp.float32)
    ).astype(jnp.bfloat16)
    gate_sum = jnp.einsum("gxcd,gxcf->xdf", routed, gate_delta, preferred_element_type=jnp.float32)
    up_sum = jnp.einsum("gxcd,gxcf->xdf", routed, up_delta, preferred_element_type=jnp.float32)
    return (grad_routed, gate_sum, up_sum, down_sum)


def orthogonal(matrix):
    is_tall = matrix.shape[-2] > matrix.shape[-1]
    iterate = jnp.swapaxes(matrix, -1, -2) if is_tall else matrix
    frobenius = jnp.sqrt(jnp.sum(iterate * iterate, axis=(-2, -1), keepdims=True))
    iterate = iterate / (frobenius + 1e-07)
    for iteration in range(NS_ITERS):
        gram_matrix = jnp.einsum(
            "...ij,...kj->...ik",
            iterate,
            iterate,
            precision=highest,
            preferred_element_type=jnp.float32,
        )
        polynomial = newton_second * gram_matrix + newton_third * jnp.einsum(
            "...ij,...jk->...ik",
            gram_matrix,
            gram_matrix,
            precision=highest,
            preferred_element_type=jnp.float32,
        )
        iterate = newton_first * iterate + jnp.einsum(
            "...ij,...jk->...ik",
            polynomial,
            iterate,
            precision=highest,
            preferred_element_type=jnp.float32,
        )
    return jnp.swapaxes(iterate, -1, -2) if is_tall else iterate


def matrix_update(moment):
    step_scale = rate_matrix * math.sqrt(max(1.0, moment.shape[-1] / moment.shape[-2]))
    return -step_scale * orthogonal(moment)


def owner_branch(chosen):

    def runner(matrices):
        return tuple(
            (
                (
                    matrix_update(matrices[position])
                    if position == chosen
                    else jnp.zeros_like(matrices[position])
                )
                for position in range(4)
            )
        )

    return runner


def local(
    tokens,
    sequence_start,
    routes,
    route_weights,
    cotangent,
    query_proj,
    key_proj,
    value_proj,
    out_proj,
    prenorm,
    midnorm,
    gate_proj,
    up_proj,
    down_proj,
    query_moment,
    key_moment,
    value_moment,
    out_moment,
    prenorm_moment,
    midnorm_moment,
    gate_moment,
    up_moment,
    down_moment,
):
    full_query, full_key, full_value, full_out, prenorm_low, midnorm_low = (
        lax.all_gather(query_proj, "shard", axis=0, tiled=True),
        lax.all_gather(key_proj, "shard", axis=0, tiled=True),
        lax.all_gather(value_proj, "shard", axis=0, tiled=True),
        lax.all_gather(out_proj, "shard", axis=0, tiled=True),
        lax.all_gather(prenorm, "shard", axis=0, tiled=True),
        lax.all_gather(midnorm, "shard", axis=0, tiled=True),
    )
    gain_before = prenorm_low.astype(jnp.float32)
    gain_after = midnorm_low.astype(jnp.float32)
    group_size = NHEADS // KVHEADS
    token_count = tokens.shape[0]
    route_count = token_count * TOPK
    inputs = tokens.astype(jnp.float32)
    scaled_first, inverse_first = root_scale(inputs)
    normed_first = (scaled_first * gain_before).astype(jnp.bfloat16)
    query_linear = jnp.dot(normed_first, full_query, preferred_element_type=jnp.float32).reshape(
        token_count, NHEADS, HEAD
    )
    key_linear = jnp.dot(normed_first, full_key, preferred_element_type=jnp.float32).reshape(
        token_count, KVHEADS, HEAD
    )
    values = (
        jnp.dot(normed_first, full_value, preferred_element_type=jnp.float32)
        .astype(jnp.bfloat16)
        .reshape(token_count, KVHEADS, HEAD)
    )
    cosine_table, sine_table = rotary_tables(
        jnp.arange(token_count, dtype=jnp.int32) - sequence_start
    )
    queries = (
        (query_linear * cosine_table + rotate_half(query_linear) * sine_table)
        .astype(jnp.bfloat16)
        .reshape(token_count, KVHEADS, group_size, HEAD)
    )
    rotated_keys = (key_linear * cosine_table + rotate_half(key_linear) * sine_table).astype(
        jnp.bfloat16
    )
    head_out, log_total = attend_forward(queries, rotated_keys, values, sequence_start)
    head_low = head_out.astype(jnp.bfloat16)
    middle = inputs + jnp.dot(head_low, full_out, preferred_element_type=jnp.float32)
    scaled_second, inverse_second = root_scale(middle)
    normed_second = (scaled_second * gain_after).astype(jnp.bfloat16)
    flat_routes = routes.reshape(route_count)
    onehot = (flat_routes[:, None] == jnp.arange(EXPERTS, dtype=jnp.int32)[None, :]).astype(
        jnp.int32
    )
    slot_rank = jnp.sum((jnp.cumsum(onehot, axis=0) - onehot) * onehot, axis=1)
    slot_place = flat_routes * CAP + slot_rank
    slot_route = (
        jnp.full((EXPERTS * CAP,), route_count, jnp.int32)
        .at[slot_place]
        .set(jnp.arange(route_count, dtype=jnp.int32))
    )
    slot_token = slot_route // TOPK
    zero_row = jnp.zeros((1, normed_second.shape[1]), jnp.bfloat16)
    send_rows = jnp.concatenate([normed_second, zero_row], axis=0)[slot_token]
    shard_count = lax.axis_size("shard")
    routed = lax.all_to_all(send_rows, "shard", split_axis=0, concat_axis=0, tiled=True).reshape(
        shard_count, gate_proj.shape[0], CAP, -1
    )
    gate_linear, up_linear, hidden, expert_out = expert_forward(
        routed, gate_proj, up_proj, down_proj
    )
    returned = lax.all_to_all(
        expert_out.reshape(EXPERTS * CAP, -1), "shard", split_axis=0, concat_axis=0, tiled=True
    )
    picked = returned[slot_place].reshape(token_count, TOPK, -1)
    mixed = middle + jnp.sum(route_weights[:, :, None] * picked.astype(jnp.float32), axis=1)
    grad_mixed = cotangent.astype(jnp.float32)
    grad_routes = (
        (route_weights[:, :, None] * grad_mixed[:, None, :])
        .astype(jnp.bfloat16)
        .reshape(route_count, -1)
    )
    grad_send = jnp.concatenate([grad_routes, zero_row], axis=0)[slot_route]
    grad_arrived = lax.all_to_all(
        grad_send, "shard", split_axis=0, concat_axis=0, tiled=True
    ).reshape(routed.shape)
    grad_routed, gate_sum, up_sum, down_sum = expert_backward(
        routed, gate_linear, up_linear, hidden, grad_arrived, gate_proj, up_proj, down_proj
    )
    grad_returned = lax.all_to_all(
        grad_routed.reshape(EXPERTS * CAP, -1), "shard", split_axis=0, concat_axis=0, tiled=True
    )
    grad_second = jnp.sum(
        grad_returned[slot_place].reshape(token_count, TOPK, -1).astype(jnp.float32), axis=1
    )
    middle_extra, midnorm_part = root_back(grad_second, gain_after, scaled_second, inverse_second)
    grad_middle = grad_mixed + middle_extra
    grad_branch = grad_middle.astype(jnp.bfloat16)
    out_local = jnp.einsum("tq,td->qd", head_low, grad_branch, preferred_element_type=jnp.float32)
    grad_heads = (
        jnp.einsum("td,qd->tq", grad_branch, full_out, preferred_element_type=jnp.float32)
        .astype(jnp.bfloat16)
        .reshape(queries.shape)
    )
    grad_queries, grad_keys, grad_values = attend_backward(
        queries, rotated_keys, values, sequence_start, log_total, grad_heads
    )
    grad_queries = grad_queries.reshape(token_count, NHEADS, HEAD)
    query_delta = (
        (grad_queries * cosine_table + rotate_back(grad_queries * sine_table))
        .astype(jnp.bfloat16)
        .reshape(token_count, -1)
    )
    key_delta = (
        (grad_keys * cosine_table + rotate_back(grad_keys * sine_table))
        .astype(jnp.bfloat16)
        .reshape(token_count, -1)
    )
    value_delta = grad_values.astype(jnp.bfloat16).reshape(token_count, -1)
    query_local = jnp.einsum(
        "td,tq->dq", normed_first, query_delta, preferred_element_type=jnp.float32
    )
    key_local = jnp.einsum("td,tq->dq", normed_first, key_delta, preferred_element_type=jnp.float32)
    value_local = jnp.einsum(
        "td,tq->dq", normed_first, value_delta, preferred_element_type=jnp.float32
    )
    grad_first = (
        jnp.einsum("tq,dq->td", query_delta, full_query, preferred_element_type=jnp.float32)
        + jnp.einsum("tq,dq->td", key_delta, full_key, preferred_element_type=jnp.float32)
        + jnp.einsum("tq,dq->td", value_delta, full_value, preferred_element_type=jnp.float32)
    )
    input_extra, prenorm_part = root_back(grad_first, gain_before, scaled_first, inverse_first)
    grad_tokens = grad_middle + input_extra
    shares = (
        lax.psum_scatter(query_local, "shard", scatter_dimension=0, tiled=True),
        lax.psum_scatter(key_local, "shard", scatter_dimension=0, tiled=True),
        lax.psum_scatter(value_local, "shard", scatter_dimension=0, tiled=True),
        lax.psum_scatter(out_local, "shard", scatter_dimension=0, tiled=True),
        lax.psum_scatter(prenorm_part, "shard", scatter_dimension=0, tiled=True),
        lax.psum_scatter(midnorm_part, "shard", scatter_dimension=0, tiled=True),
    )
    summed = lax.psum(
        (
            shares[0],
            shares[1],
            shares[2],
            shares[3],
            shares[4],
            shares[5],
            gate_sum,
            up_sum,
            down_sum,
        ),
        "rep",
    )
    (
        query_grad,
        key_grad,
        value_grad,
        out_grad,
        prenorm_grad,
        midnorm_grad,
        gate_grad,
        up_grad,
        down_grad,
    ) = summed
    query_next = momentum_keep * query_moment + query_grad
    key_next = momentum_keep * key_moment + key_grad
    value_next = momentum_keep * value_moment + value_grad
    out_next = momentum_keep * out_moment + out_grad
    prenorm_next = momentum_keep * prenorm_moment + prenorm_grad
    midnorm_next = momentum_keep * midnorm_moment + midnorm_grad
    gate_next = momentum_keep * gate_moment + gate_grad
    up_next = momentum_keep * up_moment + up_grad
    down_next = momentum_keep * down_moment + down_grad
    prenorm_update = -rate_gain * prenorm_next
    midnorm_update = -rate_gain * midnorm_next
    gate_update = matrix_update(gate_next)
    up_update = matrix_update(up_next)
    down_update = matrix_update(down_next)
    whole_states = (
        lax.all_gather(query_next, "shard", axis=0, tiled=True),
        lax.all_gather(key_next, "shard", axis=0, tiled=True),
        lax.all_gather(value_next, "shard", axis=0, tiled=True),
        lax.all_gather(out_next, "shard", axis=0, tiled=True),
    )
    my_index = lax.axis_index("shard")
    branch_list = [
        owner_branch(0),
        owner_branch(1),
        owner_branch(2),
        owner_branch(3),
        owner_branch(4),
    ]
    whole_updates = lax.switch(jnp.minimum(my_index, 4), branch_list, whole_states)
    query_update, key_update, value_update, out_update = (
        lax.psum_scatter(whole_updates[0], "shard", scatter_dimension=0, tiled=True),
        lax.psum_scatter(whole_updates[1], "shard", scatter_dimension=0, tiled=True),
        lax.psum_scatter(whole_updates[2], "shard", scatter_dimension=0, tiled=True),
        lax.psum_scatter(whole_updates[3], "shard", scatter_dimension=0, tiled=True),
    )
    return (
        mixed.astype(jnp.bfloat16),
        grad_tokens,
        query_grad,
        query_next,
        query_update,
        key_grad,
        key_next,
        key_update,
        value_grad,
        value_next,
        value_update,
        out_grad,
        out_next,
        out_update,
        prenorm_grad,
        prenorm_next,
        prenorm_update,
        midnorm_grad,
        midnorm_next,
        midnorm_update,
        gate_grad,
        gate_next,
        gate_update,
        up_grad,
        up_next,
        up_update,
        down_grad,
        down_next,
        down_update,
    )


def solution(mesh):
    return jax.shard_map(
        local,
        mesh=mesh,
        in_specs=(
            P(("rep", "shard"), None),
            P(("rep", "shard")),
            P(("rep", "shard"), None),
            P(("rep", "shard"), None),
            P(("rep", "shard"), None),
            P("shard", None),
            P("shard", None),
            P("shard", None),
            P("shard", None),
            P("shard"),
            P("shard"),
            P("shard", None, None),
            P("shard", None, None),
            P("shard", None, None),
            P("shard", None),
            P("shard", None),
            P("shard", None),
            P("shard", None),
            P("shard"),
            P("shard"),
            P("shard", None, None),
            P("shard", None, None),
            P("shard", None, None),
        ),
        out_specs=(
            P(("rep", "shard"), None),
            P(("rep", "shard"), None),
            P("shard", None),
            P("shard", None),
            P("shard", None),
            P("shard", None),
            P("shard", None),
            P("shard", None),
            P("shard", None),
            P("shard", None),
            P("shard", None),
            P("shard", None),
            P("shard", None),
            P("shard", None),
            P("shard"),
            P("shard"),
            P("shard"),
            P("shard"),
            P("shard"),
            P("shard"),
            P("shard", None, None),
            P("shard", None, None),
            P("shard", None, None),
            P("shard", None, None),
            P("shard", None, None),
            P("shard", None, None),
            P("shard", None, None),
            P("shard", None, None),
            P("shard", None, None),
        ),
        check_vma=False,
    )
```

profile of v0, /device:TPU:0, one launch (start us, length us, event | category | flops | bytes accessed | tf_op | source)
XLA Modules:
  0.0 2055.1 jit_solution(13046045805972481570)
XLA Ops:
  15.9 12.7 all-gather.1
  52.8 16.7 all-gather.13.cloned.1.call-done
  71.4 45.1 %all-gather.15.cloned.1.call-done = bf16[1024,1024]{1,0:T(8,128)(2,1)} async-done(((bf16[256,1024]{1,0:T(8,128)(2,1)}), bf16[1024,1024]{1,0:T(8,128)(2,1)}) %all-gather.15.cloned.1.call-update) | async-done | bytes 2097168 | tf_op jit(solution)/shard_map/all_gather | solution.py:252
  123.8 38.7 %all-gather.17.cloned.1.call-done = bf16[1024,1024]{1,0:T(8,128)(2,1)} async-done(((bf16[256,1024]{1,0:T(8,128)(2,1)}), bf16[1024,1024]{1,0:T(8,128)(2,1)}) %all-gather.17.cloned.1.call-update) | async-done | bytes 2097168 | tf_op jit(solution)/shard_map/all_gather | solution.py:255
  183.7 14.8 gather_fusion.2
  198.5 97.6 %all-to-all-done = bf16[4,640,1024]{2,1,0:T(8,128)(2,1)} async-done(((bf16[4,640,1024]{2,1,0:T(8,128)(2,1)}), bf16[4,640,1024]{2,1,0:T(8,128)(2,1)}, u32[]{:S(2)}, u32[]{:S(2)}) %all-to-all-start) | async-done | bytes 5242912 | tf_op jit(solution)/shard_map/all_to_all | solution.py:309
  317.7 99.0 %all-to-all-done.2 = bf16[4,640,1024]{2,1,0:T(8,128)(2,1)} async-done(((bf16[4,640,1024]{2,1,0:T(8,128)(2,1)}), bf16[4,640,1024]{2,1,0:T(8,128)(2,1)}, u32[]{:S(2)}, u32[]{:S(2)}) %all-to-all-start.2) | async-done | bytes 5242912 | tf_op jit(solution)/shard_map/all_to_all | solution.py:327
  416.7 11.1 fusion.73
  458.8 95.6 %all-to-all-done.1 = bf16[4,640,1024]{2,1,0:T(8,128)(2,1)} async-done(((bf16[4,640,1024]{2,1,0:T(8,128)(2,1)}), bf16[4,640,1024]{2,1,0:T(8,128)(2,1)}, u32[]{:S(2)}, u32[]{:S(2)}) %all-to-all-start.1) | async-done | bytes 5242912 | tf_op jit(solution)/shard_map/all_to_all | solution.py:315
  559.5 11.7 reduce-scatter.13.cloned.1.call-start
  571.2 14.1 gather_fusion.1
  590.1 84.5 %all-to-all-done.3 = bf16[4,640,1024]{2,1,0:T(8,128)(2,1)} async-done(((bf16[4,640,1024]{2,1,0:T(8,128)(2,1)}), bf16[4,640,1024]{2,1,0:T(8,128)(2,1)}, u32[]{:S(2)}, u32[]{:S(2)}) %all-to-all-start.3) | async-done | bytes 5242912 | tf_op jit(solution)/shard_map/all_to_all | solution.py:333
  674.6 14.1 gather_fusion.3
  718.8 10.3 fusion.130
  729.1 9.1 convolution_bitcast_fusion.1
  747.2 44.7 %reduce-scatter.11.cloned.1.call-done = f32[256,512]{1,0:T(8,128)} async-done(((f32[1024,512]{1,0:T(8,128)}), f32[256,512]{1,0:T(8,128)}) %reduce-scatter.11.cloned.1.call-update) | async-done | bytes 524304 | tf_op jit(solution)/shard_map/reduce_scatter | solution.py:379
  792.0 79.0 %reduce-scatter.15.cloned.1.call-done = f32[256,1024]{1,0:T(8,128)} async-done(((f32[1024,1024]{1,0:T(8,128)}), f32[256,1024]{1,0:T(8,128)}) %reduce-scatter.15.cloned.1.call-update) | async-done | bytes 1048592 | tf_op jit(solution)/shard_map/reduce_scatter | solution.py:381
  871.0 80.3 %reduce-scatter.9.cloned.1.call-done = f32[256,1024]{1,0:T(8,128)} async-done(((f32[1024,1024]{1,0:T(8,128)}), f32[256,1024]{1,0:T(8,128)}) %reduce-scatter.9.cloned.1.call-update) | async-done | bytes 1048592 | tf_op jit(solution)/shard_map/reduce_scatter | solution.py:378
  951.3 351.7 %all-reduce.9.cloned.1.call-done = (f32[256,1024]{1,0:T(8,128)}, f32[256,512]{1,0:T(8,128)}, f32[256,512]{1,0:T(8,128)}, f32[256,1024]{1,0:T(8,128)}, f32[4,1024...) async-done(((f32[256,1024]{1,0:T(8,128)}, f32[256,512]{1,0:T(8,128)}, f32[256,512]{1,0:T(8,128)}, f32[256,1024]{1,0:T(8,128)}, ...) | async-done | bytes 28311568 | tf_op jit(solution)/shard_map/psum | solution.py:385
  1317.6 12.5 all-reduce.6
  1330.2 12.6 all-reduce.4
  1351.7 46.9 %all-gather.23.cloned.1.call-done = f32[1024,512]{1,0:T(8,128)} async-done(((f32[256,512]{1,0:T(8,128)}), f32[1024,512]{1,0:T(8,128)}) %all-gather.23.cloned.1.call-update) | async-done | bytes 2097168 | tf_op jit(solution)/shard_map/all_gather | solution.py:427
  1398.5 81.5 %all-gather.19.cloned.1.call-done = f32[1024,1024]{1,0:T(8,128)} async-done(((f32[256,1024]{1,0:T(8,128)}), f32[1024,1024]{1,0:T(8,128)}) %all-gather.19.cloned.1.call-update) | async-done | bytes 4194320 | tf_op jit(solution)/shard_map/all_gather | solution.py:425
  1480.0 81.5 %all-gather.25.cloned.1.call-done = f32[1024,1024]{1,0:T(8,128)} async-done(((f32[256,1024]{1,0:T(8,128)}), f32[1024,1024]{1,0:T(8,128)}) %all-gather.25.cloned.1.call-update) | async-done | bytes 4194320 | tf_op jit(solution)/shard_map/all_gather | solution.py:428
  1561.5 122.5 %conditional.1 = (f32[1024,1024]{1,0:T(8,128)}, f32[1024,512]{0,1:T(8,128)}, f32[1024,512]{1,0:T(8,128)}, f32[1024,1024]{1,0:T(8,128)}) conditional(s32[]{:T(128)} %clamp.3, f32[1024,1024]{1,0:T(8,128)} %all-gather.19.cloned.1.call-done, f32[1024,512]{1,0:T(8,128)} %all-gather.21.cloned.1.call-done, ...), branch_computations={%region_21.23_spmd, %region_23.25_spmd, %region_25.27_spmd, %regio... | conditional | flops 77326188544 | bytes 96469096 | solution.py:438
  1566.5 17.7 fusion.16
  1584.2 13.9 fusion.235
  1598.2 14.5 multiply_add_fusion
  1612.7 14.6 fusion.236
  1627.3 13.9 fusion.237
  1641.2 15.8 add_multiply_fusion
  1684.1 10.9 multiply_reduce_fusion.6
  1695.0 11.0 multiply_reduce_fusion.5
  1706.0 19.3 fusion.230
  1733.7 11.0 multiply_reduce_fusion.4
  1747.8 22.5 %fusion.231 = f32[4,512,512]{2,1,0:T(8,128)} fusion(f32[4,1024,512]{2,1,0:T(8,128)} %get-tuple-element.245, f32[4]{0:T(128)S(1)} %sqrt_add_fusion.1), kind=kOutput, calls=%fused_computation.323 | convolution fusion | flops 12886999040 | bytes 12582928 | tf_op jit(solution)/shard_map/...ij,...kj->...ik/dot_general | solution.py:180
  1770.3 19.8 fusion.121
  1790.1 24.0 %fusion.134 = f32[4,512,512]{2,1,0:T(8,128)} fusion(f32[4,512,1024]{1,2,0:T(8,128)} %fusion.121, f32[4,1024,512]{2,1,0:T(8,128)S(1)} %bitcast.318, f32[4]{0:T(128)S(1)} %sqrt_add_fusion.2), kind=kOutput, calls=%fused_computation.179 | convolution fusion | flops 12891193344 | bytes 20971536 | tf_op jit(solution)/shard_map/...ij,...kj->...ik/dot_general | solution.py:180
  1814.2 12.5 fusion.243
  1835.0 18.1 fusion.166
  1860.6 17.8 fusion.113
  1878.4 24.8 %fusion.137 = f32[4,512,512]{2,1,0:T(8,128)} fusion(f32[4,512,1024]{1,2,0:T(8,128)} %fusion.113, f32[4,1024,512]{2,1,0:T(8,128)} %get-tuple-element.245, f32[4]{0:T(128)S(1)} %sqrt_add_fusion.1), kind=kOutput, calls=%fused_computation.180 | convolution fusion | flops 12891193344 | bytes 20971536 | tf_op jit(solution)/shard_map/...ij,...kj->...ik/dot_general | solution.py:180
  1903.2 22.7 %multiply_add_fusion.2 = f32[4,512,1024]{2,1,0:T(8,128)} fusion(f32[4,512,512]{2,1,0:T(8,128)S(1)} %fusion.246, f32[4,512,512]{2,1,0:T(8,128)S(1)} %fusion.166, f32[4,512,1024]{2,1,0:T(8,128)} %get-tuple-element.248, f32[4]{0:T(128)S(1)} %sqrt_add_fusion), kind=kOutput, calls=%fused_computation.96 | convolution fusion | flops 12896436224 | bytes 25165840 | tf_op jit(solution)/shard_map/...ij,...jk->...ik/dot_general | solution.py:194
  1925.9 12.7 fusion.245
  1938.7 14.4 fusion.247
  1960.4 16.8 add_multiply_fusion.2
  1977.3 25.4 %fusion.68 = f32[4,1024,512]{2,1,0:T(8,128)} fusion(f32[4,512,1024]{1,2,0:T(8,128)} %fusion.121, f32[4,512,512]{2,1,0:T(8,128)} %fusion.243, f32[4,512,512]{2,1,0:T(8,128)} %fusion.134, f32[4,1024,512]{2,1,0:T(8,128)} %get-tuple-element.242, f32[4]{0:T(128)S(1)} %sqrt_add_fusion.2), kind=kOutput, calls=%fused_computation.92 | convolution fusion | flops 12906921984 | bytes 33554448 | tf_op jit(solution)/shard_map/...ij,...jk->...ik/dot_general | solution.py:194
  2002.7 25.3 %fusion.65 = f32[4,1024,512]{2,1,0:T(8,128)} fusion(f32[4,512,1024]{1,2,0:T(8,128)} %fusion.113, f32[4,512,512]{2,1,0:T(8,128)} %fusion.245, f32[4,512,512]{2,1,0:T(8,128)} %fusion.137, f32[4,1024,512]{2,1,0:T(8,128)} %get-tuple-element.245, f32[4]{0:T(128)S(1)} %sqrt_add_fusion.1), kind=kOutput, calls=%fused_computation.87 | convolution fusion | flops 12906921984 | bytes 33554448 | tf_op jit(solution)/shard_map/...ij,...jk->...ik/dot_general | solution.py:194
  (271 shorter events, 251.4 us)
Async XLA Ops:
  7.2 43.7 %copy-start.3 = (bf16[256,1024]{1,0:T(8,128)(2,1)S(1)}, bf16[256,1024]{1,0:T(8,128)(2,1)}, u32[]{:S(2)}) copy-start(bf16[256,1024]{1,0:T(8,128)(2,1)} %param.28) | copy-start | bytes 1572868
  7.2 43.7 %all-gather.11.cloned.1.call-start = ((), (), s32[]{:S(2)}) async-start(), calls=%async_computation.12 | async-start | bytes 1310720 | tf_op jit(solution)/shard_map/all_gather | solution.py:254
  7.9 61.5 %all-gather.13.cloned.1.call-start = ((), (), s32[]{:S(2)}) async-start(), calls=%async_computation.13 | async-start | bytes 1310720 | tf_op jit(solution)/shard_map/all_gather | solution.py:253
  8.7 107.8 %all-gather.15.cloned.1.call-start = ((), (), s32[]{:S(2)}) async-start(), calls=%async_computation.14 | async-start | bytes 2621440 | tf_op jit(solution)/shard_map/all_gather | solution.py:252
  9.4 153.1 %all-gather.17.cloned.1.call-start = ((), (), s32[]{:S(2)}) async-start(), calls=%async_computation.15 | async-start | bytes 2621440 | tf_op jit(solution)/shard_map/all_gather | solution.py:255
  52.7 68.8 %copy-start.32 = (bf16[256,512]{0,1:T(8,128)(2,1)}, bf16[256,512]{0,1:T(8,128)(2,1)S(1)}, u32[]{:S(2)}) copy-start(bf16[256,512]{0,1:T(8,128)(2,1)S(1)} %copy.133) | copy-start | bytes 786436
  71.4 48.0 %copy-start.23 = (bf16[256,8,64,1]{0,2,3,1:T(8,128)(2,1)}, bf16[256,8,64,1]{0,2,3,1:T(8,128)(2,1)S(1)}, u32[]{:S(2)}) copy-start(bf16[256,8,64,1]{0,2,3,1:T(8,128)(2,1)S(1)} %fusion.188) | copy-start | bytes 786436
  123.8 41.2 %copy-start.30 = (bf16[8,64,2,256]{3,1,2,0:T(8,128)(2,1)}, bf16[8,64,2,256]{3,1,2,0:T(8,128)(2,1)S(1)}, u32[]{:S(2)}) copy-start(bf16[8,64,2,256]{3,1,2,0:T(8,128)(2,1)S(1)} %fusion.167) | copy-start | bytes 1572868
  175.0 121.2 %all-to-all-start = ((bf16[4,640,1024]{2,1,0:T(8,128)(2,1)}), bf16[4,640,1024]{2,1,0:T(8,128)(2,1)}, u32[]{:S(2)}, u32[]{:S(2)}) async-start(bf16[4,640,1024]{2,1,0:T(8,128)(2,1)} %bitcast.311), calls=%async_computation | async-start | bytes 10485760 | tf_op jit(solution)/shard_map/all_to_all | solution.py:309
  296.1 120.6 %all-to-all-start.2 = ((bf16[4,640,1024]{2,1,0:T(8,128)(2,1)}), bf16[4,640,1024]{2,1,0:T(8,128)(2,1)}, u32[]{:S(2)}, u32[]{:S(2)}) async-start(bf16[4,640,1024]{2,1,0:T(8,128)(2,1)} %bitcast.312), calls=%async_computation.2 | async-start | bytes 10485760 | tf_op jit(solution)/shard_map/all_to_all | solution.py:327
  416.7 11.1 copy-start.44
  434.2 120.2 %all-to-all-start.1 = ((bf16[4,640,1024]{2,1,0:T(8,128)(2,1)}), bf16[4,640,1024]{2,1,0:T(8,128)(2,1)}, u32[]{:S(2)}, u32[]{:S(2)}) async-start(bf16[4,640,1024]{2,1,0:T(8,128)(2,1)} %bitcast.314), calls=%async_computation.1 | async-start | bytes 10485760 | tf_op jit(solution)/shard_map/all_to_all | solution.py:315
  554.4 120.2 %all-to-all-start.3 = ((bf16[4,640,1024]{2,1,0:T(8,128)(2,1)}), bf16[4,640,1024]{2,1,0:T(8,128)(2,1)}, u32[]{:S(2)}, u32[]{:S(2)}) async-start(bf16[4,640,1024]{2,1,0:T(8,128)(2,1)} %bitcast.313), calls=%async_computation.3 | async-start | bytes 10485760 | tf_op jit(solution)/shard_map/all_to_all | solution.py:333
  559.5 187.8 %reduce-scatter.13.cloned.1.call-start = ((), (), s32[]{:S(2)}) async-start(), calls=%async_computation.20 | async-start | bytes 2621440 | tf_op jit(solution)/shard_map/reduce_scatter | solution.py:380
  702.9 89.1 %reduce-scatter.11.cloned.1.call-start = ((), (), s32[]{:S(2)}) async-start(), calls=%async_computation.18 | async-start | bytes 2621440 | tf_op jit(solution)/shard_map/reduce_scatter | solution.py:379
  710.4 160.6 %reduce-scatter.15.cloned.1.call-start = ((), (), s32[]{:S(2)}) async-start(), calls=%async_computation.22 | async-start | bytes 5242880 | tf_op jit(solution)/shard_map/reduce_scatter | solution.py:381
  714.6 236.7 %reduce-scatter.9.cloned.1.call-start = ((), (), s32[]{:S(2)}) async-start(), calls=%async_computation.16 | async-start | bytes 5242880 | tf_op jit(solution)/shard_map/reduce_scatter | solution.py:378
  718.5 584.5 %all-reduce.9.cloned.1.call-start = ((), (), s32[]{:S(2)}) async-start(), calls=%async_computation.28 | async-start | bytes 56623104 | tf_op jit(solution)/shard_map/psum | solution.py:385
  718.7 10.3 copy-start.22
  951.3 351.7 %copy-start.35 = (f32[256,512]{1,0:T(8,128)S(1)}, f32[256,512]{1,0:T(8,128)}, u32[]{:S(2)}) copy-start(f32[256,512]{1,0:T(8,128)} %param.43) | copy-start | bytes 1572868
  951.3 353.7 %copy-start.36 = (f32[256,512]{1,0:T(8,128)S(1)}, f32[256,512]{1,0:T(8,128)}, u32[]{:S(2)}) copy-start(f32[256,512]{1,0:T(8,128)} %param.44) | copy-start | bytes 1572868
  951.3 400.4 %all-gather.21.cloned.1.call-start = ((), (), s32[]{:S(2)}) async-start(), calls=%async_computation.19 | async-start | bytes 2621440 | tf_op jit(solution)/shard_map/all_gather | solution.py:426
  1305.0 93.6 %all-gather.23.cloned.1.call-start = ((), (), s32[]{:S(2)}) async-start(), calls=%async_computation.21 | async-start | bytes 2621440 | tf_op jit(solution)/shard_map/all_gather | solution.py:427
  1307.0 173.1 %all-gather.19.cloned.1.call-start = ((), (), s32[]{:S(2)}) async-start(), calls=%async_computation.17 | async-start | bytes 5242880 | tf_op jit(solution)/shard_map/all_gather | solution.py:425
  1309.9 251.6 %all-gather.25.cloned.1.call-start = ((), (), s32[]{:S(2)}) async-start(), calls=%async_computation.23 | async-start | bytes 5242880 | tf_op jit(solution)/shard_map/all_gather | solution.py:428
  1312.7 715.2 %reduce-scatter.21.cloned.1.call-start = ((), (), s32[]{:S(2)}) async-start(), calls=%async_computation.26 | async-start | bytes 2621440 | tf_op jit(solution)/shard_map/reduce_scatter | solution.py:442
  1315.3 27.6 %copy-start.40 = (f32[256]{0:T(256)S(1)}, f32[256]{0:T(256)}, u32[]{:S(2)}) copy-start(f32[256]{0:T(256)} %param.46) | copy-start | bytes 3076
  1315.3 28.1 %copy-start.41 = (f32[256]{0:T(256)S(1)}, f32[256]{0:T(256)}, u32[]{:S(2)}) copy-start(f32[256]{0:T(256)} %param.47) | copy-start | bytes 3076
  1315.3 28.7 %copy-start.10 = (f32[256,1024]{1,0:T(8,128)S(1)}, f32[256,1024]{1,0:T(8,128)}, u32[]{:S(2)}) copy-start(f32[256,1024]{1,0:T(8,128)} %copy-done.9) | copy-start | bytes 3145732
  1342.8 218.7 %copy-start.42 = (f32[256]{0:T(256)}, f32[256]{0:T(256)S(1)}, u32[]{:S(2)}) copy-start(f32[256]{0:T(256)S(1)} %get-tuple-element.235) | copy-start | bytes 3076
  1342.8 218.7 %copy-start.43 = (f32[256]{0:T(256)}, f32[256]{0:T(256)S(1)}, u32[]{:S(2)}) copy-start(f32[256]{0:T(256)S(1)} %get-tuple-element.238) | copy-start | bytes 3076
  1584.2 13.9 copy-start.18
  1684.1 343.9 %reduce-scatter.19.cloned.1.call-start = ((), (), s32[]{:S(2)}) async-start(), calls=%async_computation.25 | async-start | bytes 2621440 | tf_op jit(solution)/shard_map/reduce_scatter | solution.py:441
  1747.7 280.3 %reduce-scatter.17.cloned.1.call-start = ((), (), s32[]{:S(2)}) async-start(), calls=%async_computation.24 | async-start | bytes 5242880 | tf_op jit(solution)/shard_map/reduce_scatter | solution.py:440
  1747.7 22.6 %copy-start.6 = (f32[4,512,512]{2,1,0:T(8,128)S(1)}, f32[4,512,512]{2,1,0:T(8,128)}, u32[]{:S(2)}) copy-start(f32[4,512,512]{2,1,0:T(8,128)} %copy-done.5) | copy-start | bytes 12582916
  1747.7 22.6 %copy-start.15 = (f32[4,512,512]{2,1,0:T(8,128)S(1)}, f32[4,512,512]{2,1,0:T(8,128)}, u32[]{:S(2)}) copy-start(f32[4,512,512]{2,1,0:T(8,128)} %fusion.242) | copy-start | bytes 12582916
  1747.7 42.3 %slice-start.4 = ((s8[8388608]{0:T(1024)(128)(4,1)}), s8[4194304]{0:T(1024)(128)(4,1)S(1)}, s32[]{:S(2)}) async-start(s8[8388608]{0:T(1024)(128)(4,1)} %bitcast.317), calls=%async_computation.33 | async-start | bytes 8388608
  1770.3 19.8 slice-start.5
  1814.1 213.9 %reduce-scatter.23.cloned.1.call-start = ((), (), s32[]{:S(2)}) async-start(), calls=%async_computation.27 | async-start | bytes 5242880 | tf_op jit(solution)/shard_map/reduce_scatter | solution.py:443
  1814.2 12.5 copy-start.4
  1826.7 33.9 %slice-start.6 = ((s8[8388608]{0:T(1024)(128)(4,1)}), s8[4194304]{0:T(1024)(128)(4,1)S(1)}, s32[]{:S(2)}) async-start(s8[8388608]{0:T(1024)(128)(4,1)} %bitcast.319), calls=%async_computation.35 | async-start | bytes 8388608
  1835.0 25.6 %slice-start.7 = ((s8[8388608]{0:T(1024)(128)(4,1)}), s8[4194304]{0:T(1024)(128)(4,1)S(1)}, s32[]{:S(2)}) async-start(s8[8388608]{0:T(1024)(128)(4,1)} %bitcast.319), calls=%async_computation.36 | async-start | bytes 8388608
  1925.9 12.8 copy-start.2
  2002.6 25.4 %copy-start.17 = (f32[256,1024]{1,0:T(8,128)S(1)}, f32[256,1024]{1,0:T(8,128)}, u32[]{:S(2)}) copy-start(f32[256,1024]{1,0:T(8,128)} %get-tuple-element.223) | copy-start | bytes 3145732
  2002.6 26.4 %copy-start.27 = (f32[256,512]{1,0:T(8,128)S(1)}, f32[256,512]{1,0:T(8,128)}, u32[]{:S(2)}) copy-start(f32[256,512]{1,0:T(8,128)} %get-tuple-element.226) | copy-start | bytes 1572868
  2002.6 27.2 %copy-start.26 = (f32[256,512]{1,0:T(8,128)S(1)}, f32[256,512]{1,0:T(8,128)}, u32[]{:S(2)}) copy-start(f32[256,512]{1,0:T(8,128)} %get-tuple-element.229) | copy-start | bytes 1572868
  2028.0 11.5 slice-start.2
  2031.6 12.2 slice-start
  (27 other events, 109.9 us)
Sparse Core Ops, SparseCore 0:
  9.6 30.7 all-gather.10
  42.0 27.4 all-gather.12
  71.0 45.4 all-gather.14
  117.9 44.6 all-gather.16
  703.0 42.8 reduce-scatter.12
  748.7 43.1 reduce-scatter.10
  794.8 76.0 reduce-scatter.14
  873.9 77.2 reduce-scatter.8
  957.0 345.9 all-reduce.8
  1305.1 46.5 all-gather.20
  1353.8 44.6 all-gather.22
  1400.5 79.4 all-gather.18
  1482.2 79.2 all-gather.24
  1684.2 43.8 reduce-scatter.20
  1747.8 44.1 reduce-scatter.18
  1814.2 76.7 reduce-scatter.16
  1926.1 77.2 reduce-scatter.22
where the time goes:
time: 2060 us
  waiting for transfers between devices  1250 us (61%)
  matrix products  503 us (24%)
  local copies, waits for them, and re-layouts  109 us (5%)
  other arithmetic  73.5 us (4%)
  blocking collectives  45.5 us (2%)
  starting transfers between devices  33.3 us (2%)
  loops' own time  22.5 us (1%)
    psum x1, waiting for transfers between devices, local(): lax.psum((shares[0], shares[1], shares[2], shares[3], shares[4], shares[5...  352 us
    dot_general x8, matrix products, orthogonal(): jnp.einsum('...ij,...jk->...ik', polynomial, iterate, precision=highest,...  158 us
    dot_general x8, matrix products, orthogonal(): jnp.einsum('...ij,...kj->...ik', iterate, iterate, precision=highest, pre...  155 us
    all_to_all x1, waiting for transfers between devices, local(): lax.all_to_all(grad_send, 'shard', split_axis=0, concat_axis=0, tiled=True)  99 us
    all_to_all x1, waiting for transfers between devices, local(): lax.all_to_all(send_rows, 'shard', split_axis=0, concat_axis=0, tiled=True)  97.6 us
    all_to_all x1, waiting for transfers between devices, local(): lax.all_to_all(expert_out.reshape(EXPERTS * CAP, -1), 'shard', split_axis...  95.6 us
    dot_general x8, matrix products, orthogonal(): jnp.einsum('...ij,...jk->...ik', gram_matrix, gram_matrix, precision=high...  84.5 us
    all_to_all x1, waiting for transfers between devices, local(): lax.all_to_all(grad_routed.reshape(EXPERTS * CAP, -1), 'shard', split_axi...  84.5 us
  transfers between devices with their start and end apart: 21, of which 15 were waited for; matrix products, arithmetic and copies ran while one was open for 24% of the time, Pallas kernels for 0%

commit v1 on v0

--- a/solution.py
+++ b/solution.py
@@ -8,10 +8,8 @@
 NHEADS = 16
 KVHEADS = 8
 HEAD = 64
-TOPK = 8
 EXPERTS = 16
 NS_ITERS = 2
-CAP = 160
 BLOCK = 256
 
 
@@ -24,7 +22,6 @@
 newton_second = -4.775
 newton_third = 2.0315
 masked_score = -1e30
-highest = lax.Precision.HIGHEST
 
 
 def root_scale(values):
@@ -138,89 +135,36 @@
     return (grad_queries.reshape(queries.shape), finals[0], finals[1])
 
 
-def expert_forward(routed, gate_weight, up_weight, down_weight):
-    gate_linear = jnp.einsum(
-        "gxcd,xdf->gxcf", routed, gate_weight, preferred_element_type=jnp.float32
-    )
-    up_linear = jnp.einsum("gxcd,xdf->gxcf", routed, up_weight, preferred_element_type=jnp.float32)
-    hidden = (jax.nn.silu(gate_linear) * up_linear).astype(jnp.bfloat16)
-    expert_out = jnp.einsum(
-        "gxcf,xfd->gxcd", hidden, down_weight, preferred_element_type=jnp.float32
-    ).astype(jnp.bfloat16)
-    return (gate_linear, up_linear, hidden, expert_out)
-
-
-def expert_backward(
-    routed, gate_linear, up_linear, hidden, grad_out, gate_weight, up_weight, down_weight
-):
-    grad_hidden = jnp.einsum(
-        "gxcd,xfd->gxcf", grad_out, down_weight, preferred_element_type=jnp.float32
-    )
-    down_sum = jnp.einsum("gxcf,gxcd->xfd", hidden, grad_out, preferred_element_type=jnp.float32)
-    gate_sigmoid = jax.nn.sigmoid(gate_linear)
-    gate_delta = (
-        grad_hidden * up_linear * gate_sigmoid * (1.0 + gate_linear * (1.0 - gate_sigmoid))
-    ).astype(jnp.bfloat16)
-    up_delta = (grad_hidden * gate_linear * gate_sigmoid).astype(jnp.bfloat16)
-    grad_routed = (
-        jnp.einsum("gxcf,xdf->gxcd", gate_delta, gate_weight, preferred_element_type=jnp.float32)
-        + jnp.einsum("gxcf,xdf->gxcd", up_delta, up_weight, preferred_element_type=jnp.float32)
-    ).astype(jnp.bfloat16)
-    gate_sum = jnp.einsum("gxcd,gxcf->xdf", routed, gate_delta, preferred_element_type=jnp.float32)
-    up_sum = jnp.einsum("gxcd,gxcf->xdf", routed, up_delta, preferred_element_type=jnp.float32)
-    return (grad_routed, gate_sum, up_sum, down_sum)
+def mul(left, right, spec):
+    return jnp.einsum(
+        spec,
+        left.astype(jnp.bfloat16),
+        right.astype(jnp.bfloat16),
+        preferred_element_type=jnp.float32,
+    )
 
 
 def orthogonal(matrix):
-    is_tall = matrix.shape[-2] > matrix.shape[-1]
-    iterate = jnp.swapaxes(matrix, -1, -2) if is_tall else matrix
-    frobenius = jnp.sqrt(jnp.sum(iterate * iterate, axis=(-2, -1), keepdims=True))
-    iterate = iterate / (frobenius + 1e-07)
+    rows, columns = matrix.shape[-2:]
+    squares = jnp.sum(matrix * matrix, axis=(-2, -1), keepdims=True)
+    iterate = matrix / (jnp.sqrt(squares) + 1e-07)
     for iteration in range(NS_ITERS):
-        gram_matrix = jnp.einsum(
-            "...ij,...kj->...ik",
-            iterate,
-            iterate,
-            precision=highest,
-            preferred_element_type=jnp.float32,
-        )
-        polynomial = newton_second * gram_matrix + newton_third * jnp.einsum(
-            "...ij,...jk->...ik",
-            gram_matrix,
-            gram_matrix,
-            precision=highest,
-            preferred_element_type=jnp.float32,
-        )
-        iterate = newton_first * iterate + jnp.einsum(
-            "...ij,...jk->...ik",
-            polynomial,
-            iterate,
-            precision=highest,
-            preferred_element_type=jnp.float32,
-        )
-    return jnp.swapaxes(iterate, -1, -2) if is_tall else iterate
+        if rows > columns:
+            gram = mul(iterate, iterate, "...ki,...kj->...ij")
+        else:
+            gram = mul(iterate, iterate, "...ik,...jk->...ij")
+        polynomial = newton_second * gram + newton_third * mul(gram, gram, "...ij,...jk->...ik")
+        if rows > columns:
+            step = mul(iterate, polynomial, "...ij,...jk->...ik")
+        else:
+            step = mul(polynomial, iterate, "...ij,...jk->...ik")
+        iterate = newton_first * iterate + step
+    return iterate
 
 
 def matrix_update(moment):
     step_scale = rate_matrix * math.sqrt(max(1.0, moment.shape[-1] / moment.shape[-2]))
     return -step_scale * orthogonal(moment)
-
-
-def owner_branch(chosen):
-
-    def runner(matrices):
-        return tuple(
-            (
-                (
-                    matrix_update(matrices[position])
-                    if position == chosen
-                    else jnp.zeros_like(matrices[position])
-                )
-                for position in range(4)
-            )
-        )
-
-    return runner
 
 
 def local(
@@ -248,19 +192,40 @@
     up_moment,
     down_moment,
 ):
-    full_query, full_key, full_value, full_out, prenorm_low, midnorm_low = (
-        lax.all_gather(query_proj, "shard", axis=0, tiled=True),
-        lax.all_gather(key_proj, "shard", axis=0, tiled=True),
-        lax.all_gather(value_proj, "shard", axis=0, tiled=True),
-        lax.all_gather(out_proj, "shard", axis=0, tiled=True),
-        lax.all_gather(prenorm, "shard", axis=0, tiled=True),
-        lax.all_gather(midnorm, "shard", axis=0, tiled=True),
-    )
+    rep_index = lax.axis_index("rep")
+    shard_index = lax.axis_index("shard")
+    rep_count = lax.axis_size("rep")
+    shard_count = lax.axis_size("shard")
+    row_block = query_proj.shape[0]
+    piece_rows = row_block // rep_count
+    low_rows = jnp.concatenate([query_proj, key_proj, value_proj, out_proj], axis=1)
+    low_piece = lax.dynamic_slice_in_dim(low_rows, rep_index * piece_rows, piece_rows, 0)
+    low_all = lax.all_gather(low_piece, ("shard", "rep"), axis=0, tiled=True)
+    full_query = low_all[:, :1024]
+    full_key = low_all[:, 1024:1536]
+    full_value = low_all[:, 1536:2048]
+    full_out = low_all[:, 2048:]
+    gains = lax.all_gather(jnp.stack([prenorm, midnorm]), "shard", axis=1, tiled=True)
+    prenorm_low = gains[0]
+    midnorm_low = gains[1]
+    experts_here = gate_proj.shape[0]
+    dense_weights = jnp.sum(
+        jnp.where(
+            routes[:, :, None] == jnp.arange(EXPERTS, dtype=jnp.int32)[None, None, :],
+            route_weights[:, :, None],
+            0.0,
+        ),
+        axis=1,
+    )
+    dense_all = lax.all_gather(dense_weights, "shard", axis=0, tiled=True)
+    expert_weights = lax.dynamic_slice_in_dim(
+        dense_all, shard_index * experts_here, experts_here, 1
+    ).T[:, :, None]
+    cotangent_all = lax.all_gather(cotangent, "shard", axis=0, tiled=True)
     gain_before = prenorm_low.astype(jnp.float32)
     gain_after = midnorm_low.astype(jnp.float32)
     group_size = NHEADS // KVHEADS
     token_count = tokens.shape[0]
-    route_count = token_count * TOPK
     inputs = tokens.astype(jnp.float32)
     scaled_first, inverse_first = root_scale(inputs)
     normed_first = (scaled_first * gain_before).astype(jnp.bfloat16)
@@ -291,51 +256,38 @@
     middle = inputs + jnp.dot(head_low, full_out, preferred_element_type=jnp.float32)
     scaled_second, inverse_second = root_scale(middle)
     normed_second = (scaled_second * gain_after).astype(jnp.bfloat16)
-    flat_routes = routes.reshape(route_count)
-    onehot = (flat_routes[:, None] == jnp.arange(EXPERTS, dtype=jnp.int32)[None, :]).astype(
-        jnp.int32
-    )
-    slot_rank = jnp.sum((jnp.cumsum(onehot, axis=0) - onehot) * onehot, axis=1)
-    slot_place = flat_routes * CAP + slot_rank
-    slot_route = (
-        jnp.full((EXPERTS * CAP,), route_count, jnp.int32)
-        .at[slot_place]
-        .set(jnp.arange(route_count, dtype=jnp.int32))
-    )
-    slot_token = slot_route // TOPK
-    zero_row = jnp.zeros((1, normed_second.shape[1]), jnp.bfloat16)
-    send_rows = jnp.concatenate([normed_second, zero_row], axis=0)[slot_token]
-    shard_count = lax.axis_size("shard")
-    routed = lax.all_to_all(send_rows, "shard", split_axis=0, concat_axis=0, tiled=True).reshape(
-        shard_count, gate_proj.shape[0], CAP, -1
-    )
-    gate_linear, up_linear, hidden, expert_out = expert_forward(
-        routed, gate_proj, up_proj, down_proj
-    )
-    returned = lax.all_to_all(
-        expert_out.reshape(EXPERTS * CAP, -1), "shard", split_axis=0, concat_axis=0, tiled=True
-    )
-    picked = returned[slot_place].reshape(token_count, TOPK, -1)
-    mixed = middle + jnp.sum(route_weights[:, :, None] * picked.astype(jnp.float32), axis=1)
+    routed = lax.all_gather(normed_second, "shard", axis=0, tiled=True)
+    gate_linear = jnp.einsum("td,xdf->xtf", routed, gate_proj, preferred_element_type=jnp.float32)
+    up_linear = jnp.einsum("td,xdf->xtf", routed, up_proj, preferred_element_type=jnp.float32)
+    gate_sigmoid = jax.nn.sigmoid(gate_linear)
+    hidden = (gate_linear * gate_sigmoid * up_linear).astype(jnp.bfloat16)
+    expert_out = jnp.einsum("xtf,xfd->xtd", hidden, down_proj, preferred_element_type=jnp.float32)
+    partial_out = jnp.sum(
+        expert_weights * expert_out.astype(jnp.bfloat16).astype(jnp.float32), axis=0
+    ).astype(jnp.bfloat16)
+    grad_out = (expert_weights * cotangent_all.astype(jnp.float32)[None]).astype(jnp.bfloat16)
+    grad_hidden = jnp.einsum("xtd,xfd->xtf", grad_out, down_proj, preferred_element_type=jnp.float32)
+    gate_delta = (
+        grad_hidden * up_linear * gate_sigmoid * (1.0 + gate_linear * (1.0 - gate_sigmoid))
+    ).astype(jnp.bfloat16)
+    up_delta = (grad_hidden * gate_linear * gate_sigmoid).astype(jnp.bfloat16)
+    grad_routed = (
+        jnp.einsum("xtf,xdf->xtd", gate_delta, gate_proj, preferred_element_type=jnp.float32)
+        + jnp.einsum("xtf,xdf->xtd", up_delta, up_proj, preferred_element_type=jnp.float32)
+    )
+    partial_grad = jnp.sum(grad_routed, axis=0).astype(jnp.bfloat16)
+    down_sum = jnp.einsum("xtf,xtd->xfd", hidden, grad_out, preferred_element_type=jnp.float32)
+    gate_sum = jnp.einsum("td,xtf->xdf", routed, gate_delta, preferred_element_type=jnp.float32)
+    up_sum = jnp.einsum("td,xtf->xdf", routed, up_delta, preferred_element_type=jnp.float32)
+    back = lax.all_to_all(partial_grad, "shard", split_axis=0, concat_axis=0, tiled=True)
+    grad_second = jnp.sum(
+        back.reshape(shard_count, token_count, -1).astype(jnp.float32), axis=0
+    )
+    back_out = lax.all_to_all(partial_out, "shard", split_axis=0, concat_axis=0, tiled=True)
+    mixed = middle + jnp.sum(
+        back_out.reshape(shard_count, token_count, -1).astype(jnp.float32), axis=0
+    )
     grad_mixed = cotangent.astype(jnp.float32)
-    grad_routes = (
-        (route_weights[:, :, None] * grad_mixed[:, None, :])
-        .astype(jnp.bfloat16)
-        .reshape(route_count, -1)
-    )
-    grad_send = jnp.concatenate([grad_routes, zero_row], axis=0)[slot_route]
-    grad_arrived = lax.all_to_all(
-        grad_send, "shard", split_axis=0, concat_axis=0, tiled=True
-    ).reshape(routed.shape)
-    grad_routed, gate_sum, up_sum, down_sum = expert_backward(
-        routed, gate_linear, up_linear, hidden, grad_arrived, gate_proj, up_proj, down_proj
-    )
-    grad_returned = lax.all_to_all(
-        grad_routed.reshape(EXPERTS * CAP, -1), "shard", split_axis=0, concat_axis=0, tiled=True
-    )
-    grad_second = jnp.sum(
-        grad_returned[slot_place].reshape(token_count, TOPK, -1).astype(jnp.float32), axis=1
-    )
     middle_extra, midnorm_part = root_back(grad_second, gain_after, scaled_second, inverse_second)
     grad_middle = grad_mixed + middle_extra
     grad_branch = grad_middle.astype(jnp.bfloat16)
@@ -374,43 +326,34 @@
     )
     input_extra, prenorm_part = root_back(grad_first, gain_before, scaled_first, inverse_first)
     grad_tokens = grad_middle + input_extra
-    shares = (
-        lax.psum_scatter(query_local, "shard", scatter_dimension=0, tiled=True),
-        lax.psum_scatter(key_local, "shard", scatter_dimension=0, tiled=True),
-        lax.psum_scatter(value_local, "shard", scatter_dimension=0, tiled=True),
-        lax.psum_scatter(out_local, "shard", scatter_dimension=0, tiled=True),
-        lax.psum_scatter(prenorm_part, "shard", scatter_dimension=0, tiled=True),
-        lax.psum_scatter(midnorm_part, "shard", scatter_dimension=0, tiled=True),
-    )
-    summed = lax.psum(
+    low_local = jnp.concatenate([query_local, key_local, value_local, out_local], axis=1)
+    low_share = lax.psum_scatter(
+        low_local.astype(jnp.bfloat16), ("shard", "rep"), scatter_dimension=0, tiled=True
+    )
+    low_grad = lax.all_gather(low_share, "rep", axis=0, tiled=True).astype(jnp.float32)
+    low_moment = jnp.concatenate([query_moment, key_moment, value_moment, out_moment], axis=1)
+    low_next = momentum_keep * low_moment + low_grad
+    next_piece = lax.dynamic_slice_in_dim(low_next, rep_index * piece_rows, piece_rows, 0)
+    next_all = lax.all_gather(
+        next_piece.astype(jnp.bfloat16), ("shard", "rep"), axis=0, tiled=True
+    ).astype(jnp.float32)
+    gains_grad = lax.psum(jnp.stack([prenorm_part, midnorm_part]), ("shard", "rep"))
+    gains_here = lax.dynamic_slice_in_dim(gains_grad, shard_index * row_block, row_block, 1)
+    prenorm_grad = gains_here[0]
+    midnorm_grad = gains_here[1]
+    gate_grad, up_grad, down_grad = lax.psum(
         (
-            shares[0],
-            shares[1],
-            shares[2],
-            shares[3],
-            shares[4],
-            shares[5],
-            gate_sum,
-            up_sum,
-            down_sum,
+            gate_sum.astype(jnp.bfloat16),
+            up_sum.astype(jnp.bfloat16),
+            down_sum.astype(jnp.bfloat16),
         ),
         "rep",
     )
-    (
-        query_grad,
-        key_grad,
-        value_grad,
-        out_grad,
-        prenorm_grad,
-        midnorm_grad,
-        gate_grad,
-        up_grad,
-        down_grad,
-    ) = summed
-    query_next = momentum_keep * query_moment + query_grad
-    key_next = momentum_keep * key_moment + key_grad
-    value_next = momentum_keep * value_moment + value_grad
-    out_next = momentum_keep * out_moment + out_grad
+    gate_grad = gate_grad.astype(jnp.float32)
+    up_grad = up_grad.astype(jnp.float32)
+    down_grad = down_grad.astype(jnp.float32)
+    query_grad, key_grad, value_grad, out_grad = jnp.split(low_grad, (1024, 1536, 2048), axis=1)
+    query_next, key_next, value_next, out_next = jnp.split(low_next, (1024, 1536, 2048), axis=1)
     prenorm_next = momentum_keep * prenorm_moment + prenorm_grad
     midnorm_next = momentum_keep * midnorm_moment + midnorm_grad
     gate_next = momentum_keep * gate_moment + gate_grad
@@ -421,26 +364,9 @@
     gate_update = matrix_update(gate_next)
     up_update = matrix_update(up_next)
     down_update = matrix_update(down_next)
-    whole_states = (
-        lax.all_gather(query_next, "shard", axis=0, tiled=True),
-        lax.all_gather(key_next, "shard", axis=0, tiled=True),
-        lax.all_gather(value_next, "shard", axis=0, tiled=True),
-        lax.all_gather(out_next, "shard", axis=0, tiled=True),
-    )
-    my_index = lax.axis_index("shard")
-    branch_list = [
-        owner_branch(0),
-        owner_branch(1),
-        owner_branch(2),
-        owner_branch(3),
-        owner_branch(4),
-    ]
-    whole_updates = lax.switch(jnp.minimum(my_index, 4), branch_list, whole_states)
     query_update, key_update, value_update, out_update = (
-        lax.psum_scatter(whole_updates[0], "shard", scatter_dimension=0, tiled=True),
-        lax.psum_scatter(whole_updates[1], "shard", scatter_dimension=0, tiled=True),
-        lax.psum_scatter(whole_updates[2], "shard", scatter_dimension=0, tiled=True),
-        lax.psum_scatter(whole_updates[3], "shard", scatter_dimension=0, tiled=True),
+        lax.dynamic_slice_in_dim(matrix_update(whole), shard_index * row_block, row_block, 0)
+        for whole in jnp.split(next_all, (1024, 1536, 2048), axis=1)
     )
     return (
         mixed.astype(jnp.bfloat16),

time: 2060 us -> 897 us (0.44)
  waiting for transfers between devices: 1250 us -> 220 us
  matrix products: 503 us -> 403 us
  starting transfers between devices: 33.3 us -> 9.58 us
  loops' own time: 22.5 us -> 0 us
    all_to_all x4 -> x2, waiting for transfers between devices: 377 us -> 39.8 us  [the longest x1 21.4 us: local(): lax.all_to_all(partial_grad, 'shard', split_axis=0, concat_axis=0, tiled=...]
    psum x1, waiting for transfers between devices: 352 us -> 62.1 us  [local(): lax.psum((gate_sum.astype(jnp.bfloat16), up_sum.astype(jnp.bfloat16), dow...]
    reduce_scatter x8 -> x1, waiting for transfers between devices: 204 us -> 0.01 us  [local(): lax.psum_scatter(low_local.astype(jnp.bfloat16), ('shard', 'rep'), scatte...]
    all_gather x8 -> x5, waiting for transfers between devices: 317 us -> 117 us  [the longest x1 55.7 us: local(): low_all = lax.all_gather(low_piece, ('shard', 'rep'), axis=0, tiled=True)]
    dot_general x33 -> x37, matrix products: 471 us -> 375 us  [the longest x28 283 us: mul(): jnp.einsum(spec, left.astype(jnp.bfloat16), right.astype(jnp.bfloat16), p...]
    unnamed x120 -> x95, local copies, waits for them, and re-layouts: 28 us -> 89 us
    gather x4 -> x0, local copies, waits for them, and re-layouts: 51.8 us -> none  [the longest x1 14.8 us: local(): grad_send = jnp.concatenate([grad_routes, zero_row], axis=0)[slot_route]]
    psum x1, blocking collectives: 12.6 us -> 38.2 us  [local(): lax.psum(jnp.stack([prenorm_part, midnorm_part]), ('shard', 'rep'))]
  transfers between devices with their start and end apart: 21 -> 9, of which waited for: 15 -> 6; matrix products, arithmetic and copies ran while one was open for 24% -> 43% of each run, Pallas kernels for 0% -> 0%
where the time goes in v1:
time: 897 us; the launch traced here: 890 us
  matrix products  403 us (45%)
  waiting for transfers between devices  220 us (25%)
  local copies, waits for them, and re-layouts  97 us (11%)
  other arithmetic  78.4 us (9%)
  blocking collectives  64.9 us (7%)
  between operations  17.9 us (2%)
  starting transfers between devices  9.58 us (1%)
    dot_general x28, matrix products, mul(): jnp.einsum(spec, left.astype(jnp.bfloat16), right.astype(jnp.bfloat16), p...  283 us
    unnamed x95, local copies, waits for them, and re-layouts  89 us
    psum x1, waiting for transfers between devices, local(): lax.psum((gate_sum.astype(jnp.bfloat16), up_sum.astype(jnp.bfloat16), dow...  62.1 us
    all_gather x1, waiting for transfers between devices, local(): low_all = lax.all_gather(low_piece, ('shard', 'rep'), axis=0, tiled=True)  55.7 us
    all_gather x1, waiting for transfers between devices, local(): routed = lax.all_gather(normed_second, 'shard', axis=0, tiled=True)  42.7 us
    psum x1, blocking collectives, local(): lax.psum(jnp.stack([prenorm_part, midnorm_part]), ('shard', 'rep'))  38.2 us
    reduce_sum x4, other arithmetic, orthogonal(): squares = jnp.sum(matrix * matrix, axis=(-2, -1), keepdims=True)  25.5 us
    all_to_all x1, waiting for transfers between devices, local(): lax.all_to_all(partial_grad, 'shard', split_axis=0, concat_axis=0, tiled=...  21.4 us
  transfers between devices with their start and end apart: 9, of which 6 were waited for; matrix products, arithmetic and copies ran while one was open for 43% of the time, Pallas kernels for 0%

profile of v1, /device:TPU:0, one launch (start us, length us, event | category | flops | bytes accessed | tf_op | source)
XLA Modules:
  0.0 890.2 jit_solution(748790849057425769)
XLA Ops:
  14.5 12.6 %all_gather.21 = bf16[2,1024]{1,0:T(2,128)(2,1)S(1)} all-gather(bf16[2,256]{1,0:T(2,128)(2,1)S(1)} %pad_maximum_fusion.4), channel_id=1, replica_groups=mesh['rep'=8,'shard'=4] {'shard'}, dimensions={1}, use_global_device_ids=true | all-gather | bytes 5120 | tf_op jit(solution)/shard_map/all_gather | solution.py:208
  28.0 55.7 %all-gather.6.cloned.1.call-done = bf16[1024,3072]{1,0:T(8,128)(2,1)} async-done(((bf16[32,3072]{1,0:T(8,128)(2,1)}), bf16[1024,3072]{1,0:T(8,128)(2,1)}) %all-gather.6.cloned.1.call-update) | async-done | bytes 6291472 | tf_op jit(solution)/shard_map/all_gather | solution.py:203
  98.0 14.1 %all_gather.23 = f32[1024,16]{0,1:T(8,128)S(1)} all-gather(f32[256,16]{0,1:T(8,128)S(1)} %select_reduce_fusion), channel_id=1, replica_groups=mesh['rep'=8,'shard'=4] {'shard'}, dimensions={0}, use_global_device_ids=true | all-gather | bytes 81920 | tf_op jit(solution)/shard_map/all_gather | solution.py:220
  112.1 18.7 %all-gather.10.cloned.1.call-done = bf16[1024,1024]{1,0:T(8,128)(2,1)} async-done(((bf16[256,1024]{1,0:T(8,128)(2,1)}), bf16[1024,1024]{1,0:T(8,128)(2,1)}) %all-gather.10.cloned.1.call-update) | async-done | bytes 2097168 | tf_op jit(solution)/shard_map/all_gather | solution.py:224
  134.8 42.7 %all-gather.8.cloned.1.call-done = bf16[1024,1024]{1,0:T(8,128)(2,1)} async-done(((bf16[256,1024]{1,0:T(8,128)(2,1)}), bf16[1024,1024]{1,0:T(8,128)(2,1)}) %all-gather.8.cloned.1.call-update) | async-done | bytes 2097168 | tf_op jit(solution)/shard_map/all_gather | solution.py:259
  177.6 10.9 %fusion.30 = f32[1024,4,512]{2,0,1:T(8,128)} fusion(bf16[4,1024,512]{2,1,0:T(8,128)(2,1)} %param.35, bf16[1024,1024]{1,0:T(8,128)(2,1)} %all-gather.8.cloned.1.call-done), kind=kOutput, calls=%fused_computation.81 | convolution fusion | flops 4294967296 | bytes 14680064 | tf_op jit(solution)/shard_map/td,xdf->xtf/dot_general | solution.py:261
  188.4 6.7 fusion.32
  195.1 16.4 %fusion.11 = (bf16[4,1024,512]{2,1,0:T(8,128)(2,1)}, bf16[4,1024,512]{2,1,0:T(8,128)(2,1)}, bf16[4,1024,512]{2,1,0:T(8,128)(2,1)}) fusion(f32[1024,4,512]{2,0,1:T(8,128)} %fusion.32, f32[1024,4,512]{2,0,1:T(8,128)} %fusion.30, bf16[4,512,1024]{2,1,0:T(8,128)(2,1)} %param.36, f32[1024,1024]{1,0:T(8,128)S(1)} %copy-done.11, ...), kind=kOutput, calls=%fused_computation.20 | convolution fusion | flops 4336910336 | bytes 37765120 | tf_op jit(solution)/shard_map/xtd,xfd->xtf/dot_general | solution.py:269
  211.5 10.3 %fusion.245 = f32[4,1024,1024]{2,1,0:T(8,128)} fusion(bf16[4,1024,512]{2,1,0:T(8,128)(2,1)} %get-tuple-element.225, bf16[4,1024,512]{2,1,0:T(8,128)(2,1)S(1)} %copy-done.13), kind=kOutput, calls=%fused_computation.323 | convolution fusion | flops 4294967296 | bytes 25165824 | tf_op jit(solution)/shard_map/xtf,xdf->xtd/dot_general | solution.py:275
  221.9 12.5 %add_reduce_fusion = bf16[1024,1024]{1,0:T(8,128)(2,1)} fusion(f32[4,1024,1024]{2,1,0:T(8,128)} %fusion.245, bf16[4,1024,512]{2,1,0:T(8,128)(2,1)} %get-tuple-element.224, bf16[4,1024,512]{2,1,0:T(8,128)(2,1)} %param.35), kind=kOutput, calls=%fused_computation | convolution fusion | flops 4302307328 | bytes 27262976 | tf_op jit(solution)/shard_map/xtf,xdf->xtd/dot_general | solution.py:276
  239.1 8.7 copy.219
  247.7 8.7 copy.227
  256.4 9.8 %multiply_reduce_fusion = bf16[1024,1024]{1,0:T(8,128)(2,1)} fusion(f32[4,1024]{1,0:T(4,128)S(1)} %dynamic-slice_bitcast_fusion, bf16[4,1024,512]{2,1,0:T(8,128)(2,1)} %get-tuple-element.226, bf16[4,512,1024]{2,1,0:T(8,128)(2,1)} %param.36), kind=kOutput, calls=%fused_computation.2 | convolution fusion | flops 4310695936 | bytes 10502144 | tf_op jit(solution)/shard_map/xtf,xfd->xtd/dot_general | solution.py:264
  266.2 21.4 %all-to-all-done.1 = bf16[4,256,1024]{2,1,0:T(8,128)(2,1)} async-done(((bf16[4,256,1024]{2,1,0:T(8,128)(2,1)}), bf16[4,256,1024]{2,1,0:T(8,128)(2,1)}, u32[]{:S(2)}, u32[]{:S(2)}) %all-to-all-start.1) | async-done | bytes 2097184 | tf_op jit(solution)/shard_map/all_to_all | solution.py:282
  292.1 9.6 %convert_bitcast_fusion = bf16[4,1024,512]{1,2,0:T(8,128)(2,1)} fusion(bf16[4,1024,512]{2,1,0:T(8,128)(2,1)} %get-tuple-element.224, bf16[1024,1024]{1,0:T(8,128)(2,1)} %all-gather.8.cloned.1.call-done), kind=kOutput, calls=%fused_computation.50 | convolution fusion | flops 4297064448 | bytes 10485760 | tf_op jit(solution)/shard_map/td,xtf->xdf/dot_general | solution.py:281
  301.7 6.2 convert_bitcast_fusion.1
  307.9 8.9 %fusion.25 = bf16[4,512,1024]{2,1,0:T(8,128)(2,1)} fusion(bf16[4,1024,512]{2,1,0:T(8,128)(2,1)} %get-tuple-element.226, f32[1024,1024]{1,0:T(8,128)S(1)} %copy-done.12, f32[4,1024]{1,0:T(4,128)S(1)} %dynamic-slice_bitcast_fusion), kind=kOutput, calls=%fused_computation.77 | convolution fusion | flops 4305453056 | bytes 12599296 | tf_op jit(solution)/shard_map/xtf,xtd->xfd/dot_general | solution.py:279
  321.4 18.4 %all-to-all-done = bf16[4,256,1024]{2,1,0:T(8,128)(2,1)} async-done(((bf16[4,256,1024]{2,1,0:T(8,128)(2,1)}), bf16[4,256,1024]{2,1,0:T(8,128)(2,1)}, u32[]{:S(2)}, u32[]{:S(2)}) %all-to-all-start) | async-done | bytes 2097184 | tf_op jit(solution)/shard_map/all_to_all | solution.py:286
  359.0 15.6 %pad_maximum_fusion = bf16[1024,3072]{0,1:T(8,128)(2,1)} fusion(bf16[1024,1024]{0,1:T(8,128)(2,1)S(1)} %convolution_convert_fusion.1, bf16[1024,512]{0,1:T(8,128)(2,1)S(1)} %convolution_convert_fusion.2, bf16[1024,512]{0,1:T(8,128)(2,1)S(1)} %convolution_convert_fusion.3, bf16[1024,1024]{0,1:T(8,128)(2,1)S(1)} %convolution_convert_fusion), kind=kLoop, calls=%fused_computation.37 | loop fusion | flops 25165824 | bytes 12582912 | tf_op jit(solution)/shard_map/concatenate | solution.py:329
  374.6 8.7 copy.266
  389.9 38.2 %psum.28 = f32[2,1024]{1,0:T(2,128)S(1)} all-reduce(f32[2,1024]{1,0:T(2,128)S(1)} %pad_maximum_fusion.3), channel_id=1, replica_groups=mesh['rep'=8,'shard'=4] {'shard','rep'}, use_global_device_ids=true, to_apply=%region_19.20 | all-reduce | flops 2048 | bytes 16384 | tf_op jit(solution)/shard_map/psum | solution.py:340
  430.7 62.1 %all-reduce.3.cloned.1.call-done = (bf16[4,1024,512]{1,2,0:T(8,128)(2,1)}, bf16[4,1024,512]{1,2,0:T(8,128)(2,1)}, bf16[4,512,1024]{2,1,0:T(8,128)(2,1)}) async-done(((bf16[4,1024,512]{1,2,0:T(8,128)(2,1)}, bf16[4,1024,512]{1,2,0:T(8,128)(2,1)}, bf16[4,512,1024]{2,1,0:T(8,128)(2,1)}), (bf16[4,1024,512]{1,2,0:T(8,128)(2,1)}, bf16[4,1024,512]{1,2,0:T(8,128)(2,1)}, ...) | async-done | bytes 12582928 | tf_op jit(solution)/shard_map/psum | solution.py:344
  492.8 13.1 %multiply_reduce_fusion.2 = (f32[4]{0:T(128)S(1)}, f32[4,1024,512]{1,2,0:T(8,128)}, f32[4]{0:T(128)S(1)}, f32[4,1024,512]{1,2,0:T(8,128)S(1)}) fusion(bf16[4,1024,512]{1,2,0:T(8,128)(2,1)} %get-tuple-element.211, f32[4,1024,512]{1,2,0:T(8,128)} %copy.227, bf16[4,1024,512]{1,2,0:T(8,128)(2,1)} %get-tuple-element.210, f32[4,1024,512]{1,2,0:T(8,128)} %copy.219), kind=kLoop, calls=%fused_computation.27 | loop fusion | flops 20971512 | bytes 41943072 | tf_op jit(solution)/shard_map/reduce_sum | solution.py:149
  513.7 7.1 copy.235
  520.7 7.1 copy.238
  527.8 8.8 copy.236
  536.7 14.7 %fusion.48 = f32[4,1024,512]{1,2,0:T(8,128)} fusion(f32[4,512,512]{2,1,0:T(8,128)} %fusion.50, f32[4,1024,512]{1,2,0:T(8,128)} %copy-done.3, f32[4]{0:T(128)S(1)} %sqrt_add_fusion.2), kind=kOutput, calls=%fused_computation.99 | convolution fusion | flops 3230662656 | bytes 20971536 | tf_op jit(solution)/shard_map/...ij,...jk->...ik/dot_general | solution.py:139
  551.4 13.6 %fusion.217 = f32[4,512,512]{2,1,0:T(8,128)} fusion(f32[4,1024,512]{1,2,0:T(8,128)} %fusion.48, f32[4,1024,512]{1,2,0:T(8,128)} %copy-done.3, f32[4]{0:T(128)S(1)} %sqrt_add_fusion.2), kind=kOutput, calls=%fused_computation.310 | convolution fusion | flops 2155872256 | bytes 20971536 | tf_op jit(solution)/shard_map/...ki,...kj->...ij/dot_general | solution.py:139
  565.0 23.8 %add_multiply_fusion.2 = f32[4,1024,512]{1,2,0:T(8,128)} fusion(f32[4,1024,512]{1,2,0:T(8,128)} %fusion.48, f32[4,512,512]{2,1,0:T(8,128)} %fusion.217, f32[4,1024,512]{1,2,0:T(8,128)} %copy-done.3, f32[4]{0:T(128)S(1)} %sqrt_add_fusion.2), kind=kOutput, calls=%fused_computation.29 | convolution fusion | flops 3247439872 | bytes 29360144 | tf_op jit(solution)/shard_map/...ij,...jk->...ik/dot_general | solution.py:139
  588.8 8.7 copy.237
  597.5 8.7 copy.239
  606.2 10.3 %fusion.44 = f32[4,512,512]{2,1,0:T(8,128)} fusion(f32[4,1024,512]{1,2,0:T(8,128)} %get-tuple-element.217, f32[4]{0:T(128)S(1)} %sqrt_add_fusion.1), kind=kOutput, calls=%fused_computation.95 | convolution fusion | flops 2151677952 | bytes 12582928 | tf_op jit(solution)/shard_map/...ki,...kj->...ij/dot_general | solution.py:139
  616.6 14.4 %fusion.42 = f32[4,1024,512]{1,2,0:T(8,128)} fusion(f32[4,512,512]{2,1,0:T(8,128)} %fusion.44, f32[4,1024,512]{1,2,0:T(8,128)} %get-tuple-element.217, f32[4]{0:T(128)S(1)} %sqrt_add_fusion.1), kind=kOutput, calls=%fused_computation.93 | convolution fusion | flops 3230662656 | bytes 20971536 | tf_op jit(solution)/shard_map/...ij,...jk->...ik/dot_general | solution.py:139
  631.0 14.7 %fusion.214 = f32[4,512,512]{2,1,0:T(8,128)} fusion(f32[4,1024,512]{1,2,0:T(8,128)} %fusion.42, f32[4,1024,512]{1,2,0:T(8,128)} %get-tuple-element.217, f32[4]{0:T(128)S(1)} %sqrt_add_fusion.1), kind=kOutput, calls=%fused_computation.309 | convolution fusion | flops 2155872256 | bytes 20971536 | tf_op jit(solution)/shard_map/...ki,...kj->...ij/dot_general | solution.py:139
  650.0 23.4 %add_multiply_fusion.1 = f32[4,1024,512]{1,2,0:T(8,128)} fusion(f32[4,1024,512]{1,2,0:T(8,128)} %fusion.42, f32[4,512,512]{2,1,0:T(8,128)} %fusion.214, f32[4,1024,512]{1,2,0:T(8,128)} %get-tuple-element.217, f32[4]{0:T(128)S(1)} %sqrt_add_fusion.1), kind=kOutput, calls=%fused_computation.25 | convolution fusion | flops 3247439872 | bytes 29360144 | tf_op jit(solution)/shard_map/...ij,...jk->...ik/dot_general | solution.py:139
  673.4 8.7 copy.240
  682.1 9.1 %multiply_reduce_fusion.1 = (f32[4]{0:T(128)S(1)}, f32[4,512,1024]{2,1,0:T(8,128)S(1)}, f32[4,512,1024]{2,1,0:T(8,128)}) fusion(f32[4,512,1024]{2,1,0:T(8,128)} %param.45, bf16[4,512,1024]{2,1,0:T(8,128)(2,1)} %get-tuple-element.212), kind=kLoop, calls=%fused_computation.23 | loop fusion | flops 10485756 | bytes 29360144 | tf_op jit(solution)/shard_map/reduce_sum | solution.py:149
  699.1 14.1 %fusion.36 = f32[4,512,1024]{2,1,0:T(8,128)} fusion(f32[4,512,512]{2,1,0:T(8,128)} %fusion.38, f32[4,512,1024]{2,1,0:T(8,128)} %copy-done.10, f32[4]{0:T(128)S(1)} %sqrt_add_fusion), kind=kOutput, calls=%fused_computation.87 | convolution fusion | flops 3230662656 | bytes 20971536 | tf_op jit(solution)/shard_map/...ij,...jk->...ik/dot_general | solution.py:139
  713.2 14.1 %fusion.211 = f32[4,512,512]{2,1,0:T(8,128)} fusion(f32[4,512,1024]{2,1,0:T(8,128)} %fusion.36, f32[4,512,1024]{2,1,0:T(8,128)} %copy-done.10, f32[4]{0:T(128)S(1)} %sqrt_add_fusion), kind=kOutput, calls=%fused_computation.308 | convolution fusion | flops 2155872256 | bytes 20971536 | tf_op jit(solution)/shard_map/...ik,...jk->...ij/dot_general | solution.py:139
  727.4 21.1 %add_multiply_fusion = f32[4,512,1024]{2,1,0:T(8,128)} fusion(f32[4,512,1024]{2,1,0:T(8,128)} %fusion.36, f32[4,512,512]{2,1,0:T(8,128)} %fusion.211, f32[4,512,1024]{2,1,0:T(8,128)} %copy-done.10, f32[4]{0:T(128)S(1)} %sqrt_add_fusion), kind=kOutput, calls=%fused_computation.21 | convolution fusion | flops 3247439872 | bytes 29360144 | tf_op jit(solution)/shard_map/...ij,...jk->...ik/dot_general | solution.py:139
  790.2 8.0 fusion.232
  798.2 14.2 %multiply_add_fusion.6 = f32[1024,1024]{1,0:T(8,128)} fusion(f32[]{:T(128)S(6)} %add.284, f32[1024,3072]{1,0:T(8,128)} %copy-done.2, f32[1024,1024]{1,0:T(8,128)} %fusion.232), kind=kOutput, calls=%fused_computation.57 | convolution fusion | flops 4305453056 | bytes 20972544 | tf_op jit(solution)/shard_map/...ij,...jk->...ik/dot_general | solution.py:139
  812.5 7.8 fusion.113
  820.3 12.7 %fusion.111 = f32[1024,1024]{1,0:T(8,128)} fusion(f32[1024,1024]{1,0:T(8,128)} %multiply_add_fusion.6, f32[1024,1024]{1,0:T(8,128)} %fusion.113), kind=kOutput, calls=%fused_computation.185 | convolution fusion | flops 4301258752 | bytes 12582912 | tf_op jit(solution)/shard_map/...ij,...jk->...ik/dot_general | solution.py:139
  833.0 8.1 fusion.235
  841.1 14.3 %multiply_add_fusion.7 = f32[1024,1024]{1,0:T(8,128)} fusion(f32[]{:T(128)S(6)} %add.268, f32[1024,3072]{1,0:T(8,128)} %copy-done.2, f32[1024,1024]{1,0:T(8,128)} %fusion.235), kind=kOutput, calls=%fused_computation.61 | convolution fusion | flops 4305453056 | bytes 20972544 | tf_op jit(solution)/shard_map/...ij,...jk->...ik/dot_general | solution.py:139
  855.3 8.1 fusion.121
  863.4 12.9 %fusion.119 = f32[1024,1024]{1,0:T(8,128)} fusion(f32[1024,1024]{1,0:T(8,128)} %multiply_add_fusion.7, f32[1024,1024]{1,0:T(8,128)} %fusion.121), kind=kOutput, calls=%fused_computation.193 | convolution fusion | flops 4301258752 | bytes 12582912 | tf_op jit(solution)/shard_map/...ij,...jk->...ik/dot_general | solution.py:139
  (187 shorter events, 133.7 us)
Async XLA Ops:
  7.2 79.3 %copy-start.4 = (bf16[256,1024]{1,0:T(8,128)(2,1)S(1)}, bf16[256,1024]{1,0:T(8,128)(2,1)}, u32[]{:S(2)}) copy-start(bf16[256,1024]{1,0:T(8,128)(2,1)} %param.23) | copy-start | bytes 1572868
  7.2 76.5 %all-gather.6.cloned.1.call-start = ((), (), s32[]{:S(2)}) async-start(), calls=%async_computation.3 | async-start | bytes 6488064 | tf_op jit(solution)/shard_map/all_gather | solution.py:203
  8.9 121.8 %all-gather.10.cloned.1.call-start = ((), (), s32[]{:S(2)}) async-start(), calls=%async_computation.5 | async-start | bytes 2621440 | tf_op jit(solution)/shard_map/all_gather | solution.py:224
  9.7 167.9 %all-gather.8.cloned.1.call-start = ((), (), s32[]{:S(2)}) async-start(), calls=%async_computation.4 | async-start | bytes 2621440 | tf_op jit(solution)/shard_map/all_gather | solution.py:259
  14.5 74.0 %copy-start.31 = (f32[256]{0:T(256)}, f32[256]{0:T(256)S(1)}, u32[]{:S(2)}) copy-start(f32[256]{0:T(256)S(1)} %add_rsqrt_fusion.1) | copy-start | bytes 3076
  27.1 61.3 %copy-start.28 = (f32[1,1024]{1,0:T(1,128)}, f32[1,1024]{1,0:T(1,128)S(1)}, u32[]{:S(2)}) copy-start(f32[1,1024]{1,0:T(1,128)S(1)} %get-tuple-element.252) | copy-start | bytes 12292
  27.1 69.8 %copy-start.30 = (f32[1,1024]{1,0:T(1,128)}, f32[1,1024]{1,0:T(1,128)S(1)}, u32[]{:S(2)}) copy-start(f32[1,1024]{1,0:T(1,128)S(1)} %get-tuple-element.251) | copy-start | bytes 12292
  88.5 3.0 copy-start.25
  91.4 1.4 copy-start.21
  92.2 2.0 copy-start
  94.3 40.6 %copy-start.15 = (bf16[8,64,2,256]{3,1,2,0:T(8,128)(2,1)}, bf16[8,64,2,256]{3,1,2,0:T(8,128)(2,1)S(1)}, u32[]{:S(2)}) copy-start(bf16[8,64,2,256]{3,1,2,0:T(8,128)(2,1)S(1)} %fusion.86) | copy-start | bytes 1572868
  94.3 3.7 copy-start.35
  94.3 3.7 copy-start.36
  96.9 1.0 copy-start.34
  177.6 10.9 %copy-start.13 = (bf16[4,1024,512]{2,1,0:T(8,128)(2,1)S(1)}, bf16[4,1024,512]{2,1,0:T(8,128)(2,1)}, u32[]{:S(2)}) copy-start(bf16[4,1024,512]{2,1,0:T(8,128)(2,1)} %param.34) | copy-start | bytes 12582916
  177.6 10.9 %copy-start.41 = (bf16[1024,1024]{1,0:T(8,128)(2,1)S(1)}, bf16[1024,1024]{1,0:T(8,128)(2,1)}, u32[]{:S(2)}) copy-start(bf16[1024,1024]{1,0:T(8,128)(2,1)} %all-gather.8.cloned.1.call-done) | copy-start | bytes 6291460
  188.4 6.7 copy-start.11
  234.4 53.2 %all-to-all-start.1 = ((bf16[4,256,1024]{2,1,0:T(8,128)(2,1)}), bf16[4,256,1024]{2,1,0:T(8,128)(2,1)}, u32[]{:S(2)}, u32[]{:S(2)}) async-start(bf16[4,256,1024]{2,1,0:T(8,128)(2,1)} %bitcast.164), calls=%async_computation.1 | async-start | bytes 4194304 | tf_op jit(solution)/shard_map/all_to_all | solution.py:282
  287.6 52.3 %all-to-all-start = ((bf16[4,256,1024]{2,1,0:T(8,128)(2,1)}), bf16[4,256,1024]{2,1,0:T(8,128)(2,1)}, u32[]{:S(2)}, u32[]{:S(2)}) async-start(bf16[4,256,1024]{2,1,0:T(8,128)(2,1)} %bitcast.163), calls=%async_computation | async-start | bytes 4194304 | tf_op jit(solution)/shard_map/all_to_all | solution.py:286
  292.0 200.7 %all-reduce.3.cloned.1.call-start = ((), (), s32[]{:S(2)}) async-start(), calls=%async_computation.9 | async-start | bytes 25165824 | tf_op jit(solution)/shard_map/psum | solution.py:344
  292.1 9.6 %copy-start.14 = (bf16[4,1024,512]{2,1,0:T(8,128)(2,1)S(1)}, bf16[4,1024,512]{2,1,0:T(8,128)(2,1)}, u32[]{:S(2)}) copy-start(bf16[4,1024,512]{2,1,0:T(8,128)(2,1)} %get-tuple-element.225) | copy-start | bytes 12582916
  292.1 9.6 %copy-start.42 = (bf16[1024,1024]{1,0:T(8,128)(2,1)S(1)}, bf16[1024,1024]{1,0:T(8,128)(2,1)}, u32[]{:S(2)}) copy-start(bf16[1024,1024]{1,0:T(8,128)(2,1)} %all-gather.8.cloned.1.call-done) | copy-start | bytes 6291460
  301.7 6.2 copy-start.12
  316.8 299.7 %reduce-scatter.4.cloned.1.call-start = ((), (), s32[]{:S(2)}) async-start(), calls=%async_computation.8 | async-start | bytes 6488064 | tf_op jit(solution)/shard_map/reduce_scatter | solution.py:330
  344.3 3.6 copy-start.22
  348.0 4.2 copy-start.1
  354.1 1.3 copy-start.27
  354.2 3.2 copy-start.17
  355.3 1.0 copy-start.29
  355.3 1.0 copy-start.32
  356.3 2.0 copy-start.9
  356.3 2.0 copy-start.16
  374.6 8.7 copy-start.18
  386.1 3.7 copy-start.33
  428.1 2.0 copy-start.39
  428.1 2.0 copy-start.40
  429.4 216.3 %all-gather.12.cloned.1.call-start = ((), (), s32[]{:S(2)}) async-start(), calls=%async_computation.6 | async-start | bytes 1769472 | tf_op jit(solution)/shard_map/all_gather | solution.py:333
  505.8 3.4 copy-start.3
  616.6 136.8 %all-gather.14.cloned.1.call-start = ((), (), s32[]{:S(2)}) async-start(), calls=%async_computation.7 | async-start | bytes 6488064 | tf_op jit(solution)/shard_map/all_gather | solution.py:337
  631.0 14.7 %copy-start.19 = (f32[256,1024]{1,0:T(8,128)S(1)}, f32[256,1024]{1,0:T(8,128)}, u32[]{:S(2)}) copy-start(f32[256,1024]{1,0:T(8,128)} %param.40) | copy-start | bytes 3145732
  631.0 14.7 %copy-start.20 = (f32[256,1024]{1,0:T(8,128)S(1)}, f32[256,1024]{1,0:T(8,128)}, u32[]{:S(2)}) copy-start(f32[256,1024]{1,0:T(8,128)} %param.37) | copy-start | bytes 3145732
  631.0 14.7 %copy-start.23 = (f32[256,512]{1,0:T(8,128)S(1)}, f32[256,512]{1,0:T(8,128)}, u32[]{:S(2)}) copy-start(f32[256,512]{1,0:T(8,128)} %param.39) | copy-start | bytes 1572868
  631.0 14.7 %copy-start.24 = (f32[256,512]{1,0:T(8,128)S(1)}, f32[256,512]{1,0:T(8,128)}, u32[]{:S(2)}) copy-start(f32[256,512]{1,0:T(8,128)} %param.38) | copy-start | bytes 1572868
  647.6 1.7 copy-start.6
  691.3 3.4 copy-start.10
  727.4 21.1 %copy-start.5 = (bf16[256,3072]{1,0:T(8,128)(2,1)S(1)}, bf16[256,3072]{1,0:T(8,128)(2,1)}, u32[]{:S(2)}) copy-start(bf16[256,3072]{1,0:T(8,128)(2,1)} %all-gather.12.cloned.1.call-done) | copy-start | bytes 4718596
  748.5 2.7 copy-start.7
  757.8 4.5 copy-start.2
  (4 other events, 2.9 us)
Sparse Core Ops, SparseCore 0:
  11.5 72.1 all-gather.5
  85.3 45.3 all-gather.9
  132.9 44.6 all-gather.7
  317.0 175.7 all-reduce.2
  499.2 114.3 reduce-scatter.3
  616.7 26.0 all-gather.11
  650.1 69.8 all-gather.13

commit v2 on v1

--- a/solution.py
+++ b/solution.py
@@ -1,8 +1,11 @@
+import functools
 import math
 
 import jax
 import jax.numpy as jnp
 from jax import lax
+from jax.experimental import pallas as pl
+from jax.experimental.pallas import tpu as pltpu
 from jax.sharding import PartitionSpec as P
 
 NHEADS = 16
@@ -135,36 +138,107 @@
     return (grad_queries.reshape(queries.shape), finals[0], finals[1])
 
 
-def mul(left, right, spec):
-    return jnp.einsum(
-        spec,
-        left.astype(jnp.bfloat16),
-        right.astype(jnp.bfloat16),
-        preferred_element_type=jnp.float32,
-    )
-
-
-def orthogonal(matrix):
-    rows, columns = matrix.shape[-2:]
-    squares = jnp.sum(matrix * matrix, axis=(-2, -1), keepdims=True)
-    iterate = matrix / (jnp.sqrt(squares) + 1e-07)
-    for iteration in range(NS_ITERS):
-        if rows > columns:
-            gram = mul(iterate, iterate, "...ki,...kj->...ij")
-        else:
-            gram = mul(iterate, iterate, "...ik,...jk->...ij")
-        polynomial = newton_second * gram + newton_third * mul(gram, gram, "...ij,...jk->...ik")
-        if rows > columns:
-            step = mul(iterate, polynomial, "...ij,...jk->...ik")
-        else:
-            step = mul(polynomial, iterate, "...ij,...jk->...ik")
-        iterate = newton_first * iterate + step
-    return iterate
-
-
-def matrix_update(moment):
-    step_scale = rate_matrix * math.sqrt(max(1.0, moment.shape[-1] / moment.shape[-2]))
-    return -step_scale * orthogonal(moment)
+def newton_parts(gram):
+    a, b, c = newton_first, newton_second, newton_third
+
+    def times(left, right):
+        return jnp.dot(left, right, preferred_element_type=jnp.float32)
+
+    low = gram.astype(jnp.bfloat16)
+    first = b * gram + c * times(low, low)
+    first_low = first.astype(jnp.bfloat16)
+    mixed_term = times(low, first_low)
+    second_gram = (a * a) * gram + (2.0 * a) * mixed_term + times(
+        mixed_term.astype(jnp.bfloat16), first_low
+    )
+    second_low = second_gram.astype(jnp.bfloat16)
+    second = b * second_gram + c * times(second_low, second_low)
+    return (first, first_low, second, second.astype(jnp.bfloat16))
+
+
+def expert_update_kernel(tall, scale, grad_ref, moment_ref, grad_out, next_out, update_out):
+    a = newton_first
+    grad = grad_ref[0].astype(jnp.float32)
+    moment = momentum_keep * moment_ref[0] + grad
+    grad_out[0] = grad
+    next_out[0] = moment
+    inverse = 1.0 / (jnp.sqrt(jnp.sum(moment * moment)) + 1e-07)
+    low = (moment * inverse).astype(jnp.bfloat16)
+    sides = (((0,), (0,)), ((), ())) if tall else (((1,), (1,)), ((), ()))
+    gram = lax.dot_general(low, low, sides, preferred_element_type=jnp.float32)
+    first, first_low, second, second_low = newton_parts(gram)
+    rest = a * (first + second) + jnp.dot(
+        first_low, second_low, preferred_element_type=jnp.float32
+    )
+    rest = rest.astype(jnp.bfloat16)
+    if tall:
+        step = jnp.dot(low, rest, preferred_element_type=jnp.float32)
+    else:
+        step = jnp.dot(rest, low, preferred_element_type=jnp.float32)
+    update_out[0] = (-scale * a * a * inverse) * next_out[0] - scale * step
+
+
+def expert_update(grad, moment):
+    count, rows, columns = moment.shape
+    scale = rate_matrix * math.sqrt(max(1.0, columns / rows))
+    block = pl.BlockSpec((1, rows, columns), lambda i: (i, 0, 0))
+    shape = jax.ShapeDtypeStruct(moment.shape, jnp.float32)
+    return pl.pallas_call(
+        functools.partial(expert_update_kernel, rows > columns, scale),
+        grid=(count,),
+        in_specs=[block, block],
+        out_specs=[block, block, block],
+        out_shape=[shape, shape, shape],
+        compiler_params=pltpu.CompilerParams(vmem_limit_bytes=56 * 1024 * 1024),
+        name="expert_update",
+        cost_estimate=pl.CostEstimate(
+            flops=count * 2500000000, bytes_accessed=moment.size * 18, transcendentals=0
+        ),
+    )(grad, moment)
+
+
+def dense_update_kernel(layout, start_ref, whole_ref, *outs):
+    a = newton_first
+    block_rows = outs[0].shape[0]
+    start = pl.multiple_of(start_ref[0] * block_rows, block_rows)
+    for (begin, width), out in zip(layout, outs):
+        columns = pl.ds(begin, width)
+        matrix = whole_ref[:, columns].astype(jnp.float32)
+        scale = rate_matrix * math.sqrt(max(1.0, width / matrix.shape[0]))
+        inverse = 1.0 / (jnp.sqrt(jnp.sum(matrix * matrix)) + 1e-07)
+        low = (matrix * inverse).astype(jnp.bfloat16)
+        gram = lax.dot_general(
+            low, low, (((0,), (0,)), ((), ())), preferred_element_type=jnp.float32
+        )
+        first, first_low, second, second_low = newton_parts(gram)
+        own = whole_ref[pl.ds(start, block_rows), columns].astype(jnp.float32) * inverse
+        once = a * own + jnp.dot(
+            own.astype(jnp.bfloat16), first_low, preferred_element_type=jnp.float32
+        )
+        out[...] = (-scale) * (
+            a * once
+            + jnp.dot(once.astype(jnp.bfloat16), second_low, preferred_element_type=jnp.float32)
+        )
+
+
+def dense_update(whole, layout, shard_index, block_rows):
+    return pl.pallas_call(
+        functools.partial(dense_update_kernel, layout),
+        in_specs=[
+            pl.BlockSpec(memory_space=pltpu.SMEM),
+            pl.BlockSpec(memory_space=pltpu.VMEM),
+        ],
+        out_specs=[pl.BlockSpec(memory_space=pltpu.VMEM)] * len(layout),
+        out_shape=[jax.ShapeDtypeStruct((block_rows, width), jnp.float32) for _, width in layout],
+        compiler_params=pltpu.CompilerParams(vmem_limit_bytes=60 * 1024 * 1024),
+        name="dense_update",
+        cost_estimate=pl.CostEstimate(
+            flops=28000000000, bytes_accessed=whole.size * 3, transcendentals=0
+        ),
+    )(shard_index.reshape(1).astype(jnp.int32), whole)
+
+
+LAYOUT = ((0, 1024), (1024, 512), (1536, 512), (2048, 1024))
 
 
 def local(
@@ -336,7 +410,7 @@
     next_piece = lax.dynamic_slice_in_dim(low_next, rep_index * piece_rows, piece_rows, 0)
     next_all = lax.all_gather(
         next_piece.astype(jnp.bfloat16), ("shard", "rep"), axis=0, tiled=True
-    ).astype(jnp.float32)
+    )
     gains_grad = lax.psum(jnp.stack([prenorm_part, midnorm_part]), ("shard", "rep"))
     gains_here = lax.dynamic_slice_in_dim(gains_grad, shard_index * row_block, row_block, 1)
     prenorm_grad = gains_here[0]
@@ -349,25 +423,18 @@
         ),
         "rep",
     )
-    gate_grad = gate_grad.astype(jnp.float32)
-    up_grad = up_grad.astype(jnp.float32)
-    down_grad = down_grad.astype(jnp.float32)
     query_grad, key_grad, value_grad, out_grad = jnp.split(low_grad, (1024, 1536, 2048), axis=1)
     query_next, key_next, value_next, out_next = jnp.split(low_next, (1024, 1536, 2048), axis=1)
     prenorm_next = momentum_keep * prenorm_moment + prenorm_grad
     midnorm_next = momentum_keep * midnorm_moment + midnorm_grad
-    gate_next = momentum_keep * gate_moment + gate_grad
-    up_next = momentum_keep * up_moment + up_grad
-    down_next = momentum_keep * down_moment + down_grad
     prenorm_update = -rate_gain * prenorm_next
     midnorm_update = -rate_gain * midnorm_next
-    gate_update = matrix_update(gate_next)
-    up_update = matrix_update(up_next)
-    down_update = matrix_update(down_next)
-    query_update, key_update, value_update, out_update = (
-        lax.dynamic_slice_in_dim(matrix_update(whole), shard_index * row_block, row_block, 0)
-        for whole in jnp.split(next_all, (1024, 1536, 2048), axis=1)
-    )
+    query_update, key_update, value_update, out_update = dense_update(
+        next_all, LAYOUT, shard_index, row_block
+    )
+    gate_grad, gate_next, gate_update = expert_update(gate_grad, gate_moment)
+    up_grad, up_next, up_update = expert_update(up_grad, up_moment)
+    down_grad, down_next, down_update = expert_update(down_grad, down_moment)
     return (
         mixed.astype(jnp.bfloat16),
         grad_tokens,

time: 897 us -> 805 us (0.90)
  matrix products: 403 us -> 118 us
  waiting for transfers between devices: 220 us -> 452 us
  Pallas kernels: 0 us -> 97.6 us
  local copies, waits for them, and re-layouts: 97 us -> 11.1 us
  other arithmetic: 78.4 us -> 27.6 us
    dot_general x28 -> x0, matrix products: 283 us -> none  [mul(): jnp.einsum(spec, left.astype(jnp.bfloat16), right.astype(jnp.bfloat16), p...]
    reduce_scatter x1, waiting for transfers between devices: 0.01 us -> 113 us  [local(): lax.psum_scatter(low_local.astype(jnp.bfloat16), ('shard', 'rep'), scatte...]
    pallas_call x0 -> x4, Pallas kernels: none -> 97.6 us  [the longest x3 61.5 us: expert_update(): pl.pallas_call(functools.partial(expert_update_kernel, rows > columns, sc...]
    unnamed x95 -> x82, local copies, waits for them, and re-layouts: 89 us -> 4.18 us
    psum x1, waiting for transfers between devices: 62.1 us -> 126 us  [local(): lax.psum((gate_sum.astype(jnp.bfloat16), up_sum.astype(jnp.bfloat16), dow...]
    all_to_all x1, waiting for transfers between devices: 18.4 us -> 44.8 us  [local(): lax.all_to_all(partial_out, 'shard', split_axis=0, concat_axis=0, tiled=T...]
    reduce_sum x4 -> x0, other arithmetic: 25.5 us -> none  [orthogonal(): squares = jnp.sum(matrix * matrix, axis=(-2, -1), keepdims=True)]
    all_to_all x1, waiting for transfers between devices: 21.4 us -> 38.7 us  [local(): lax.all_to_all(partial_grad, 'shard', split_axis=0, concat_axis=0, tiled=...]
  transfers between devices with their start and end apart: 9 -> 9, of which waited for: 6 -> 9; matrix products, arithmetic and copies ran while one was open for 43% -> 9% of each run, Pallas kernels for 0% -> 8%
where the time goes in v2:
time: 805 us; the launch traced here: 799 us
  waiting for transfers between devices  452 us (56%)
  matrix products  118 us (15%)
  Pallas kernels  97.6 us (12%)
  blocking collectives  67.1 us (8%)
  other arithmetic  27.6 us (3%)
  between operations  15 us (2%)
  local copies, waits for them, and re-layouts  11.1 us (1%)
  starting transfers between devices  9.81 us (1%)
    psum x1, waiting for transfers between devices, local(): lax.psum((gate_sum.astype(jnp.bfloat16), up_sum.astype(jnp.bfloat16), dow...  126 us
    reduce_scatter x1, waiting for transfers between devices, local(): lax.psum_scatter(low_local.astype(jnp.bfloat16), ('shard', 'rep'), scatte...  113 us
    pallas_call x3, Pallas kernels, expert_update(): pl.pallas_call(functools.partial(expert_update_kernel, rows > columns, sc...  61.5 us
    all_gather x1, waiting for transfers between devices, local(): low_all = lax.all_gather(low_piece, ('shard', 'rep'), axis=0, tiled=True)  56.2 us
    all_to_all x1, waiting for transfers between devices, local(): lax.all_to_all(partial_out, 'shard', split_axis=0, concat_axis=0, tiled=T...  44.8 us
    all_gather x1, waiting for transfers between devices, local(): routed = lax.all_gather(normed_second, 'shard', axis=0, tiled=True)  42.8 us
    psum x1, blocking collectives, local(): lax.psum(jnp.stack([prenorm_part, midnorm_part]), ('shard', 'rep'))  40.7 us
    all_to_all x1, waiting for transfers between devices, local(): lax.all_to_all(partial_grad, 'shard', split_axis=0, concat_axis=0, tiled=...  38.7 us
  transfers between devices with their start and end apart: 9, of which 9 were waited for; matrix products, arithmetic and copies ran while one was open for 9% of the time, Pallas kernels for 8%

profile of v2, /device:TPU:0, one launch (start us, length us, event | category | flops | bytes accessed | tf_op | source)
XLA Modules:
  0.0 798.8 jit_solution(4529694688849635282)
XLA Ops:
  7.3 1.6 fusion.82
  13.9 12.6 %all_gather.21 = bf16[2,1024]{1,0:T(2,128)(2,1)S(1)} all-gather(bf16[2,256]{1,0:T(2,128)(2,1)S(1)} %pad_maximum_fusion.4), channel_id=1, replica_groups=mesh['rep'=8,'shard'=4] {'shard'}, dimensions={1}, use_global_device_ids=true | all-gather | bytes 5120 | tf_op jit(solution)/shard_map/all_gather | solution.py:282
  27.4 56.2 %all-gather.6.cloned.1.call-done = bf16[1024,3072]{1,0:T(8,128)(2,1)} async-done(((bf16[32,3072]{1,0:T(8,128)(2,1)}), bf16[1024,3072]{1,0:T(8,128)(2,1)}) %all-gather.6.cloned.1.call-update) | async-done | bytes 6291472 | tf_op jit(solution)/shard_map/all_gather | solution.py:277
  83.6 1.9 convolution_convert_fusion.4
  85.6 1.9 fusion.69
  87.7 2.7 fusion.39
  94.3 2.4 multiply_reduce_fusion.3
  97.8 13.8 %all_gather.23 = f32[1024,16]{0,1:T(8,128)S(1)} all-gather(f32[256,16]{0,1:T(8,128)S(1)} %select_reduce_fusion), channel_id=1, replica_groups=mesh['rep'=8,'shard'=4] {'shard'}, dimensions={0}, use_global_device_ids=true | all-gather | bytes 81920 | tf_op jit(solution)/shard_map/all_gather | solution.py:294
  111.6 18.9 %all-gather.10.cloned.1.call-done = bf16[1024,1024]{1,0:T(8,128)(2,1)} async-done(((bf16[256,1024]{1,0:T(8,128)(2,1)}), bf16[1024,1024]{1,0:T(8,128)(2,1)}) %all-gather.10.cloned.1.call-update) | async-done | bytes 2097168 | tf_op jit(solution)/shard_map/all_gather | solution.py:298
  130.6 4.1 convert_element_type.154
  134.7 42.8 %all-gather.8.cloned.1.call-done = bf16[1024,1024]{1,0:T(8,128)(2,1)} async-done(((bf16[256,1024]{1,0:T(8,128)(2,1)}), bf16[1024,1024]{1,0:T(8,128)(2,1)}) %all-gather.8.cloned.1.call-update) | async-done | bytes 2097168 | tf_op jit(solution)/shard_map/all_gather | solution.py:333
  177.4 10.9 %fusion.27 = f32[1024,4,512]{2,0,1:T(8,128)} fusion(bf16[4,1024,512]{2,1,0:T(8,128)(2,1)} %param.35, bf16[1024,1024]{1,0:T(8,128)(2,1)} %all-gather.8.cloned.1.call-done), kind=kOutput, calls=%fused_computation.47 | convolution fusion | flops 4294967296 | bytes 14680064 | tf_op jit(solution)/shard_map/td,xdf->xtf/dot_general | solution.py:335
  188.3 6.7 fusion.29
  195.0 16.4 %fusion.11 = (bf16[4,1024,512]{2,1,0:T(8,128)(2,1)}, bf16[4,1024,512]{2,1,0:T(8,128)(2,1)}, bf16[4,1024,512]{2,1,0:T(8,128)(2,1)}) fusion(f32[1024,4,512]{2,0,1:T(8,128)} %fusion.29, f32[1024,4,512]{2,0,1:T(8,128)} %fusion.27, bf16[4,512,1024]{2,1,0:T(8,128)(2,1)} %param.36, f32[1024,1024]{1,0:T(8,128)S(1)} %copy-done.10, ...), kind=kOutput, calls=%fused_computation.20 | convolution fusion | flops 4336910336 | bytes 37765120 | tf_op jit(solution)/shard_map/xtd,xfd->xtf/dot_general | solution.py:343
  211.4 10.5 %fusion.99 = f32[4,1024,1024]{2,1,0:T(8,128)} fusion(bf16[4,1024,512]{2,1,0:T(8,128)(2,1)} %get-tuple-element.124, bf16[4,1024,512]{2,1,0:T(8,128)(2,1)S(1)} %copy-done.12), kind=kOutput, calls=%fused_computation.163 | convolution fusion | flops 4294967296 | bytes 25165824 | tf_op jit(solution)/shard_map/xtf,xdf->xtd/dot_general | solution.py:349
  221.9 11.6 %add_reduce_fusion = bf16[1024,1024]{1,0:T(8,128)(2,1)} fusion(f32[4,1024,1024]{2,1,0:T(8,128)} %fusion.99, bf16[4,1024,512]{2,1,0:T(8,128)(2,1)} %get-tuple-element.123, bf16[4,1024,512]{2,1,0:T(8,128)(2,1)S(1)} %copy-done.38), kind=kOutput, calls=%fused_computation | convolution fusion | flops 4302307328 | bytes 27262976 | tf_op jit(solution)/shard_map/xtf,xdf->xtd/dot_general | solution.py:350
  233.5 4.9 all-to-all-start.1
  238.4 9.8 %multiply_reduce_fusion = bf16[1024,1024]{1,0:T(8,128)(2,1)} fusion(f32[4,1024]{1,0:T(4,128)S(1)} %dynamic-slice_bitcast_fusion, bf16[4,1024,512]{2,1,0:T(8,128)(2,1)} %get-tuple-element.125, bf16[4,512,1024]{2,1,0:T(8,128)(2,1)} %param.36), kind=kOutput, calls=%fused_computation.2 | convolution fusion | flops 4310695936 | bytes 10502144 | tf_op jit(solution)/shard_map/xtf,xfd->xtd/dot_general | solution.py:338
  248.2 38.7 %all-to-all-done.1 = bf16[4,256,1024]{2,1,0:T(8,128)(2,1)} async-done(((bf16[4,256,1024]{2,1,0:T(8,128)(2,1)}), bf16[4,256,1024]{2,1,0:T(8,128)(2,1)}, u32[]{:S(2)}, u32[]{:S(2)}) %all-to-all-start.1) | async-done | bytes 2097184 | tf_op jit(solution)/shard_map/all_to_all | solution.py:356
  286.9 4.5 all-to-all-start
  291.5 2.1 convert_reduce_fusion
  294.5 44.8 %all-to-all-done = bf16[4,256,1024]{2,1,0:T(8,128)(2,1)} async-done(((bf16[4,256,1024]{2,1,0:T(8,128)(2,1)}), bf16[4,256,1024]{2,1,0:T(8,128)(2,1)}, u32[]{:S(2)}, u32[]{:S(2)}) %all-to-all-start) | async-done | bytes 2097184 | tf_op jit(solution)/shard_map/all_to_all | solution.py:360
  339.2 2.1 convert_reduce_fusion.1
  341.3 2.2 multiply_add_fusion
  344.5 3.2 fusion.48
  349.0 3.1 fusion.54
  352.4 1.9 fusion.16
  359.8 3.0 pad_maximum_fusion
  362.9 113.4 %reduce-scatter.2.cloned.1.call-done = bf16[32,3072]{1,0:T(8,128)(2,1)} async-done(((bf16[1024,3072]{1,0:T(8,128)(2,1)}), bf16[32,3072]{1,0:T(8,128)(2,1)}) %reduce-scatter.2.cloned.1.call-update) | async-done | bytes 196624 | tf_op jit(solution)/shard_map/reduce_scatter | solution.py:404
  476.6 8.6 %convert_bitcast_fusion = bf16[4,1024,512]{2,1,0:T(8,128)(2,1)} fusion(bf16[4,1024,512]{2,1,0:T(8,128)(2,1)} %get-tuple-element.123, bf16[1024,1024]{1,0:T(8,128)(2,1)S(1)} %copy-done.40), kind=kOutput, calls=%fused_computation.32 | convolution fusion | flops 4297064448 | bytes 10485760 | tf_op jit(solution)/shard_map/td,xtf->xdf/dot_general | solution.py:355
  485.1 6.2 convert_bitcast_fusion.1
  491.4 8.9 %fusion.22 = bf16[4,512,1024]{2,1,0:T(8,128)(2,1)} fusion(bf16[4,1024,512]{2,1,0:T(8,128)(2,1)} %get-tuple-element.125, f32[1024,1024]{1,0:T(8,128)S(1)} %copy-done.11, f32[4,1024]{1,0:T(4,128)S(1)} %copy-done.31), kind=kOutput, calls=%fused_computation.43 | convolution fusion | flops 4305453056 | bytes 12599296 | tf_op jit(solution)/shard_map/xtf,xtd->xfd/dot_general | solution.py:353
  500.4 2.7 all-gather.12.cloned.1.call-done
  503.1 2.3 fusion.21
  505.5 1.8 copy-done.4
  508.0 2.3 fusion.37
  510.4 1.8 convolution_add_fusion.1
  512.2 2.0 fusion.62
  514.2 40.7 %psum.28 = f32[2,1024]{1,0:T(2,128)S(1)} all-reduce(f32[2,1024]{1,0:T(2,128)S(1)} %pad_maximum_fusion.3), channel_id=1, replica_groups=mesh['rep'=8,'shard'=4] {'shard','rep'}, use_global_device_ids=true, to_apply=%region_15.16 | all-reduce | flops 2048 | bytes 16384 | tf_op jit(solution)/shard_map/psum | solution.py:414
  555.6 1.3 fusion.61
  556.9 125.7 %all-reduce.3.cloned.1.call-done = (bf16[4,1024,512]{2,1,0:T(8,128)(2,1)}, bf16[4,1024,512]{2,1,0:T(8,128)(2,1)}, bf16[4,512,1024]{2,1,0:T(8,128)(2,1)}) async-done(((bf16[4,1024,512]{2,1,0:T(8,128)(2,1)}, bf16[4,1024,512]{2,1,0:T(8,128)(2,1)}, bf16[4,512,1024]{2,1,0:T(8,128)(2,1)}), (bf16[4,1024,512]{2,1,0:T(8,128)(2,1)}, bf16[4,1024,512]{2,1,0:T(8,128)(2,1)}, ...) | async-done | bytes 12582928 | tf_op jit(solution)/shard_map/psum | solution.py:418
  682.5 20.4 %expert_update.3 = (f32[4,1024,512]{2,1,0:T(8,128)}, f32[4,1024,512]{2,1,0:T(8,128)}, f32[4,1024,512]{2,1,0:T(8,128)}) custom-call(bf16[4,1024,512]{2,1,0:T(8,128)(2,1)} %get-tuple-element.116.grad_ref, f32[4,1024,512]{2,1,0:T(8,128)} %moment_ref.3), custom_call_target="tpu_custom_call" | custom-call | flops 10000000000 | bytes 37748736 | tf_op jit(solution)/shard_map/expert_update/pallas_call | solution.py:186
  702.9 20.4 %expert_update.4 = (f32[4,1024,512]{2,1,0:T(8,128)}, f32[4,1024,512]{2,1,0:T(8,128)}, f32[4,1024,512]{2,1,0:T(8,128)}) custom-call(bf16[4,1024,512]{2,1,0:T(8,128)(2,1)} %get-tuple-element.117.grad_ref, f32[4,1024,512]{2,1,0:T(8,128)} %moment_ref.4), custom_call_target="tpu_custom_call" | custom-call | flops 10000000000 | bytes 37748736 | tf_op jit(solution)/shard_map/expert_update/pallas_call | solution.py:186
  723.3 20.7 %expert_update.5 = (f32[4,512,1024]{2,1,0:T(8,128)}, f32[4,512,1024]{2,1,0:T(8,128)}, f32[4,512,1024]{2,1,0:T(8,128)}) custom-call(bf16[4,512,1024]{2,1,0:T(8,128)(2,1)} %get-tuple-element.118.grad_ref, f32[4,512,1024]{2,1,0:T(8,128)} %moment_ref.5), custom_call_target="tpu_custom_call" | custom-call | flops 10000000000 | bytes 37748736 | tf_op jit(solution)/shard_map/expert_update/pallas_call | solution.py:186
  744.1 1.4 fusion.92
  745.4 2.1 fusion.91
  747.5 8.1 %all-gather.14.cloned.1.call-done.whole_ref = bf16[1024,3072]{1,0:T(8,128)(2,1)} async-done(((bf16[32,3072]{1,0:T(8,128)(2,1)}), bf16[1024,3072]{1,0:T(8,128)(2,1)}) %all-gather.14.cloned.1.call-update) | async-done | bytes 6291472 | tf_op jit(solution)/shard_map/all_gather | solution.py:411
  755.6 36.1 %dense_update.1 = (f32[256,1024]{1,0:T(8,128)}, f32[256,512]{1,0:T(8,128)}, f32[256,512]{1,0:T(8,128)}, f32[256,1024]{1,0:T(8,128)}) custom-call(s32[1]{0:T(128)} %bitcast.42.start_ref, bf16[1024,3072]{1,0:T(8,128)(2,1)} %all-gather.14.cloned.1.call-done.whole_ref), custom_call_target="tpu_custom_call" | custom-call | flops 28000000000 | bytes 9437184 | tf_op jit(solution)/shard_map/dense_update/pallas_call | solution.py:225
  (140 shorter events, 21.6 us)
Async XLA Ops:
  7.2 78.4 %copy-start.2 = (bf16[256,1024]{1,0:T(8,128)(2,1)S(1)}, bf16[256,1024]{1,0:T(8,128)(2,1)}, u32[]{:S(2)}) copy-start(bf16[256,1024]{1,0:T(8,128)(2,1)} %param.23) | copy-start | bytes 1572868
  7.2 76.4 %all-gather.6.cloned.1.call-start = ((), (), s32[]{:S(2)}) async-start(), calls=%async_computation.3 | async-start | bytes 6488064 | tf_op jit(solution)/shard_map/all_gather | solution.py:277
  8.9 121.6 %all-gather.10.cloned.1.call-start = ((), (), s32[]{:S(2)}) async-start(), calls=%async_computation.5 | async-start | bytes 2621440 | tf_op jit(solution)/shard_map/all_gather | solution.py:298
  9.7 167.7 %all-gather.8.cloned.1.call-start = ((), (), s32[]{:S(2)}) async-start(), calls=%async_computation.4 | async-start | bytes 2621440 | tf_op jit(solution)/shard_map/all_gather | solution.py:333
  13.8 73.8 %copy-start.26 = (f32[256]{0:T(256)}, f32[256]{0:T(256)S(1)}, u32[]{:S(2)}) copy-start(f32[256]{0:T(256)S(1)} %add_rsqrt_fusion.1) | copy-start | bytes 3076
  26.5 61.2 %copy-start.23 = (f32[1,1024]{1,0:T(1,128)}, f32[1,1024]{1,0:T(1,128)S(1)}, u32[]{:S(2)}) copy-start(f32[1,1024]{1,0:T(1,128)S(1)} %get-tuple-element.151) | copy-start | bytes 12292
  85.6 7.3 copy-start.19
  87.7 3.0 copy-start.14
  92.3 2.0 copy-start
  94.3 3.4 copy-start.32
  94.3 3.5 copy-start.33
  111.6 126.8 %copy-start.30 = (f32[4,1024]{1,0:T(4,128)}, f32[4,1024]{1,0:T(4,128)S(1)}, u32[]{:S(2)}) copy-start(f32[4,1024]{1,0:T(4,128)S(1)} %dynamic-slice_bitcast_fusion) | copy-start | bytes 49156
  177.4 10.9 %copy-start.12 = (bf16[4,1024,512]{2,1,0:T(8,128)(2,1)S(1)}, bf16[4,1024,512]{2,1,0:T(8,128)(2,1)}, u32[]{:S(2)}) copy-start(bf16[4,1024,512]{2,1,0:T(8,128)(2,1)} %param.34) | copy-start | bytes 12582916
  177.4 10.9 %copy-start.39 = (bf16[1024,1024]{1,0:T(8,128)(2,1)S(1)}, bf16[1024,1024]{1,0:T(8,128)(2,1)}, u32[]{:S(2)}) copy-start(bf16[1024,1024]{1,0:T(8,128)(2,1)} %all-gather.8.cloned.1.call-done) | copy-start | bytes 6291460
  188.3 6.7 copy-start.10
  211.4 10.5 %copy-start.38 = (bf16[4,1024,512]{2,1,0:T(8,128)(2,1)S(1)}, bf16[4,1024,512]{2,1,0:T(8,128)(2,1)}, u32[]{:S(2)}) copy-start(bf16[4,1024,512]{2,1,0:T(8,128)(2,1)} %param.35) | copy-start | bytes 12582916
  233.5 53.4 %all-to-all-start.1 = ((bf16[4,256,1024]{2,1,0:T(8,128)(2,1)}), bf16[4,256,1024]{2,1,0:T(8,128)(2,1)}, u32[]{:S(2)}, u32[]{:S(2)}) async-start(bf16[4,256,1024]{2,1,0:T(8,128)(2,1)} %bitcast.164), calls=%async_computation.1 | async-start | bytes 4194304 | tf_op jit(solution)/shard_map/all_to_all | solution.py:356
  286.9 52.3 %all-to-all-start = ((bf16[4,256,1024]{2,1,0:T(8,128)(2,1)}), bf16[4,256,1024]{2,1,0:T(8,128)(2,1)}, u32[]{:S(2)}, u32[]{:S(2)}) async-start(bf16[4,256,1024]{2,1,0:T(8,128)(2,1)} %bitcast.163), calls=%async_computation | async-start | bytes 4194304 | tf_op jit(solution)/shard_map/all_to_all | solution.py:360
  291.4 184.9 %reduce-scatter.2.cloned.1.call-start = ((), (), s32[]{:S(2)}) async-start(), calls=%async_computation.6 | async-start | bytes 6488064 | tf_op jit(solution)/shard_map/reduce_scatter | solution.py:404
  343.6 1.0 copy-start.6
  348.9 3.5 copy-start.1
  352.4 1.9 copy-start.24
  352.4 1.9 copy-start.27
  355.0 1.1 copy-start.15
  355.0 1.6 copy-start.9
  355.0 1.6 copy-start.21
  357.8 1.1 copy-start.16
  362.8 113.8 %copy-start.40 = (bf16[1024,1024]{1,0:T(8,128)(2,1)S(1)}, bf16[1024,1024]{1,0:T(8,128)(2,1)}, u32[]{:S(2)}) copy-start(bf16[1024,1024]{1,0:T(8,128)(2,1)} %all-gather.8.cloned.1.call-done) | copy-start | bytes 6291460
  362.8 140.3 %all-gather.12.cloned.1.call-start = ((), (), s32[]{:S(2)}) async-start(), calls=%async_computation.7 | async-start | bytes 1769472 | tf_op jit(solution)/shard_map/all_gather | solution.py:407
  476.3 206.2 %all-reduce.3.cloned.1.call-start = ((), (), s32[]{:S(2)}) async-start(), calls=%async_computation.9 | async-start | bytes 25165824 | tf_op jit(solution)/shard_map/psum | solution.py:418
  476.6 8.6 %copy-start.13 = (bf16[4,1024,512]{2,1,0:T(8,128)(2,1)S(1)}, bf16[4,1024,512]{2,1,0:T(8,128)(2,1)}, u32[]{:S(2)}) copy-start(bf16[4,1024,512]{2,1,0:T(8,128)(2,1)} %get-tuple-element.124) | copy-start | bytes 12582916
  485.1 6.2 copy-start.11
  485.1 6.2 copy-start.31
  500.3 2.8 copy-start.18
  500.3 2.8 copy-start.20
  500.3 7.6 copy-start.17
  500.3 255.3 %all-gather.14.cloned.1.call-start = ((), (), s32[]{:S(2)}) async-start(), calls=%async_computation.8 | async-start | bytes 6488064 | tf_op jit(solution)/shard_map/all_gather | solution.py:411
  505.5 1.8 copy-start.4
  507.2 4.9 copy-start.25
  507.2 5.0 copy-start.28
  510.3 3.9 copy-start.29
  510.3 44.7 %copy-start.36 = (f32[256]{0:T(256)S(1)}, f32[256]{0:T(256)}, u32[]{:S(2)}) copy-start(f32[256]{0:T(256)} %param.42) | copy-start | bytes 3076
  510.3 44.7 %copy-start.37 = (f32[256]{0:T(256)S(1)}, f32[256]{0:T(256)}, u32[]{:S(2)}) copy-start(f32[256]{0:T(256)} %param.41) | copy-start | bytes 3076
  510.3 45.3 %copy-start.7 = (f32[256,1024]{1,0:T(8,128)S(1)}, f32[256,1024]{1,0:T(8,128)}, u32[]{:S(2)}) copy-start(f32[256,1024]{1,0:T(8,128)} %copy-done.6) | copy-start | bytes 3145732
  555.0 147.9 %copy-start.34 = (f32[1,256]{1,0:T(1,128)}, f32[1,256]{1,0:T(1,128)S(1)}, u32[]{:S(2)}) copy-start(f32[1,256]{1,0:T(1,128)S(1)} %get-tuple-element.148) | copy-start | bytes 3076
  555.0 147.9 %copy-start.35 = (f32[1,256]{1,0:T(1,128)}, f32[1,256]{1,0:T(1,128)S(1)}, u32[]{:S(2)}) copy-start(f32[1,256]{1,0:T(1,128)S(1)} %get-tuple-element.149) | copy-start | bytes 3076
  723.3 20.7 %copy-start.3 = (bf16[256,3072]{1,0:T(8,128)(2,1)S(1)}, bf16[256,3072]{1,0:T(8,128)(2,1)}, u32[]{:S(2)}) copy-start(bf16[256,3072]{1,0:T(8,128)(2,1)} %all-gather.12.cloned.1.call-done) | copy-start | bytes 4718596
  723.3 20.7 %copy-start.5 = (f32[256,3072]{1,0:T(8,128)S(1)}, f32[256,3072]{1,0:T(8,128)}, u32[]{:S(2)}) copy-start(f32[256,3072]{1,0:T(8,128)} %copy-done.4) | copy-start | bytes 9437188
  (2 other events, 1.6 us)
Sparse Core Ops, SparseCore 0:
  11.5 72.0 all-gather.5
  85.1 45.4 all-gather.9
  132.7 44.6 all-gather.7
  362.9 113.3 reduce-scatter.1
  478.2 24.8 all-gather.11
  508.0 174.4 all-reduce.2
  686.0 69.6 all-gather.13
